TPU v7x, 32 devices: a whole 2x2x4 slice. The times are simulated.
32 devices in a mesh: rep: 2 (over y), lab: 16 (over z, x, core).
Axes of the slice: x: 2, y: 2, z: 4, core: 2. Of those that a mesh axis runs over, the one named last changes fastest.
Arguments:
- queries: bfloat16 [4096, 768], P(('rep', 'lab')), may hold values from -6 to 6
- shortlist: int32 [4096, 8], P(('rep', 'lab')), may hold values from 0 to 127, all different within a row; in each aligned block of 128 rows (0 to 127, 128 to 255, ...) at most 8 rows name the same one
- positive: int32 [4096, 8], P(('rep', 'lab')), may hold values from 0 to 255
- label_weight: bfloat16 [16384, 768], P('lab'), may hold values from -0.21875 to 0.21875
- first_moment: float32 [2, 8192, 768], P('rep', 'lab'), may hold values from -6 to 6
- second_moment: float32 [2, 8192, 768], P('rep', 'lab'), may hold values from 0.5 to 8
Outputs:
- query_grad: float32 [4096, 768], P(('rep', 'lab'))
- new_weight: float32 [16384, 768], P('lab')
- new_first: float32 [2, 8192, 768], P('rep', 'lab')
- new_second: float32 [2, 8192, 768], P('rep', 'lab')
Inputs may be any that keep to these rules, and one draw needn't show every extreme that they name: `shortlist`: the 8 blocks of one query are distinct; among the 128 rows of one device (aligned blocks of rows) no block is named by more than 8 rows, and some block is named by exactly 8.
All inputs are finite; a program needn't handle non-finite values.
Results may differ from a plain program's by a relative error of at most 0.0026.
Values may be sent and summed in bfloat16 or wider, within the bound.
A program may use at most 64 MiB of HBM per device.

v0:
```python
import jax
import jax.numpy as jnp
from jax import lax
from jax.sharding import PartitionSpec as P

D = 768
BLOCK = 128
K = 8
CAP = 8


beta_first = 0.9
beta_second = 0.999
learn_rate = 0.01
adam_epsilon = 1e-08
step_count = 100.0


def send_back(row_parts, target_slot, rows_here):
    returned = lax.all_to_all(row_parts[None], "lab", split_axis=2, concat_axis=0, tiled=True)
    flat_back = returned.reshape(-1, D)
    pieces = flat_back[target_slot].reshape(rows_here, K, D)
    return jnp.sum(pieces, axis=1)


def update_shard(weight_grad, label_weight, first_moment, second_moment):
    summed = lax.psum_scatter(weight_grad, "rep", scatter_dimension=0, tiled=True)
    shard_rows = summed.shape[0]
    grad_shard = summed[None]
    new_first = beta_first * first_moment + (1.0 - beta_first) * grad_shard
    new_second = beta_second * second_moment + (1.0 - beta_second) * grad_shard * grad_shard
    first_hat = new_first / (1.0 - beta_first**step_count)
    second_hat = new_second / (1.0 - beta_second**step_count)
    step_view = first_hat / (jnp.sqrt(second_hat) + adam_epsilon)
    offset = lax.axis_index("rep") * shard_rows
    own_rows = lax.dynamic_slice_in_dim(label_weight, offset, shard_rows, 0)
    fresh_rows = own_rows.astype(jnp.float32) - learn_rate * step_view[0]
    new_weight = lax.all_gather(fresh_rows, "rep", axis=0, tiled=True)
    return (new_weight, new_first, new_second)


def body(queries, shortlist, positive, label_weight, first_moment, second_moment):
    lab_count = lax.axis_size("lab")
    rows_here = queries.shape[0]
    local_labels = label_weight.shape[0]
    blk_dev = local_labels // BLOCK
    nblk = blk_dev * lab_count
    block_ids = shortlist.reshape(-1)
    onehot = (block_ids[:, None] == jnp.arange(nblk, dtype=jnp.int32)[None, :]).astype(jnp.int32)
    before = jnp.cumsum(onehot, axis=0) - onehot
    slot_index = jnp.sum(before * onehot, axis=1)
    target_slot = block_ids * CAP + slot_index
    item_ids = jnp.arange(rows_here * K, dtype=jnp.int32)
    filler = jnp.full((nblk * CAP,), -1, jnp.int32).at[target_slot].set(item_ids)
    live_slot = filler >= 0
    safe_item = jnp.maximum(filler, 0)
    source_row = safe_item // K
    send_rows = jnp.where(live_slot[:, None], queries[source_row], jnp.zeros((), jnp.bfloat16))
    send_rows = send_rows.reshape(lab_count, blk_dev, CAP, D)
    send_marks = jnp.where(live_slot, positive.reshape(-1)[safe_item], -1).astype(jnp.bfloat16)
    send_marks = send_marks.reshape(lab_count, blk_dev, CAP)
    arrived_rows, arrived_marks = (
        lax.all_to_all(send_rows, "lab", split_axis=0, concat_axis=2, tiled=True),
        lax.all_to_all(send_marks, "lab", split_axis=0, concat_axis=2, tiled=True),
    )
    groups = 2
    arrived_rows = arrived_rows.reshape(blk_dev // groups, groups, lab_count * CAP, D)
    arrived_marks = arrived_marks.reshape(blk_dev // groups, groups, lab_count * CAP).astype(
        jnp.float32
    )
    label_tiles = label_weight.reshape(blk_dev // groups, groups, BLOCK, D)
    offsets = jnp.arange(BLOCK, dtype=jnp.float32)

    def tile_work(inputs):
        rows, marks, tiles = inputs
        logits = jnp.einsum("bsd,bld->bsl", rows, tiles, preferred_element_type=jnp.float32)
        labels = (offsets[None, None, :] == marks[:, :, None]).astype(jnp.float32)
        slopes = jnp.where(marks[:, :, None] >= 0.0, jax.nn.sigmoid(logits) - labels, 0.0).astype(
            jnp.bfloat16
        )
        row_parts = jnp.einsum("bsl,bld->bsd", slopes, tiles, preferred_element_type=jnp.float32)
        weight_parts = jnp.einsum("bsl,bsd->bld", slopes, rows, preferred_element_type=jnp.float32)
        return (row_parts, weight_parts)

    row_parts, weight_parts = lax.map(tile_work, (arrived_rows, arrived_marks, label_tiles))
    row_parts = row_parts.reshape(blk_dev, lab_count * CAP, D)
    weight_grad = weight_parts.reshape(local_labels, D)
    query_grad = send_back(row_parts, target_slot, rows_here)
    new_weight, new_first, new_second = update_shard(
        weight_grad, label_weight, first_moment, second_moment
    )
    return (query_grad, new_weight, new_first, new_second)


def solution(mesh):
    in_specs = (
        P(("rep", "lab"), None),
        P(("rep", "lab"), None),
        P(("rep", "lab"), None),
        P("lab", None),
        P("rep", "lab", None),
        P("rep", "lab", None),
    )
    out_specs = (
        P(("rep", "lab"), None),
        P("lab", None),
        P("rep", "lab", None),
        P("rep", "lab", None),
    )
    return jax.shard_map(body, mesh=mesh, in_specs=in_specs, out_specs=out_specs, check_vma=False)
```

profile of v0, /device:TPU:0, one launch (start us, length us, event | category | flops | bytes accessed | tf_op | source)
XLA Modules:
  0.0 198.4 jit_solution(2928732283691908919)
XLA Ops:
  7.2 0.8 copy.24
  8.0 0.1 eq.42
  8.2 0.7 broadcast_multiply_fusion
  8.9 0.1 copy.26
  9.0 0.2 fusion.26
  9.3 0.1 copy.27
  9.4 0.1 copy.23
  9.5 0.1 mul.67
  9.6 0.4 fusion.25
  10.0 4.3 %scatter_custom_fusion = s32[1024]{0:T(1024)S(1)} fusion(s32[1024]{0:T(1024)S(1)} %bitcast.94, s32[1024]{0:T(1024)S(1)} %iota.14, s32[]{:T(128)} %constant.33.clone.1), kind=kCustom, calls=%fused_computation.62 | custom fusion | bytes 4100 | tf_op jit(solution)/shard_map/scatter | solution.py:54
  14.3 0.1 copy.28
  14.4 0.1 reshape.107
  14.5 4.5 %gather_fusion = s32[1024]{0:T(1024)S(1)} fusion(s32[1024]{0:T(1024)S(1)} %reshape.107, s32[1024]{0:T(1024)S(1)} %get-tuple-element.78), kind=kCustom, calls=%fused_computation | custom fusion | bytes 12288 | tf_op jit(solution)/shard_map/gather | solution.py:60
  19.1 0.7 reshape.108
  19.8 7.4 %all-to-all-start = ((bf16[16,8,8]{2,1,0:T(8,128)(2,1)}), bf16[16,8,8]{2,1,0:T(8,128)(2,1)S(1)}, u32[]{:S(2)}, u32[]{:S(2)}) async-start(bf16[16,8,8]{2,1,0:T(8,128)(2,1)} %reshape.108), calls=%async_computation | async-start | bytes 65536 | tf_op jit(solution)/shard_map/all_to_all | solution.py:64
  27.2 0.1 broadcast_in_dim.56
  27.3 4.0 %gather_fusion.1 = bf16[1024,768]{1,0:T(8,128)(2,1)S(1)} fusion(bf16[128,768]{1,0:T(8,128)(2,1)S(1)} %copy-done, s32[1024]{0:T(1024)S(1)} %get-tuple-element.77), kind=kCustom, calls=%fused_computation.1 | custom fusion | bytes 3149824 | tf_op jit(solution)/shard_map/gather | solution.py:58
  31.3 1.4 broadcast_select_fusion
  32.6 1.2 all-to-all-done
  33.8 4.9 %all-to-all-start.1 = ((bf16[16,8,8,768]{3,2,1,0:T(8,128)(2,1)}), bf16[16,8,8,768]{3,2,1,0:T(8,128)(2,1)S(1)}, u32[]{:S(2)}, u32[]{:S(2)}) async-start(bf16[16,8,8,768]{3,2,1,0:T(8,128)(2,1)} %broadcast_select_fusion), calls=%async_computation.1 | async-start | bytes 3145728 | tf_op jit(solution)/shard_map/all_to_all | solution.py:63
  38.8 0.1 reshape.114
  38.9 31.8 %all-to-all-done.1 = bf16[16,8,8,768]{3,2,1,0:T(8,128)(2,1)S(1)} async-done(((bf16[16,8,8,768]{3,2,1,0:T(8,128)(2,1)}), bf16[16,8,8,768]{3,2,1,0:T(8,128)(2,1)S(1)}, u32[]{:S(2)}, u32[]{:S(2)}) %all-to-all-start.1) | async-done | bytes 1572896 | tf_op jit(solution)/shard_map/all_to_all | solution.py:63
  70.6 0.1 copy.30
  70.7 18.5 %while.13 = (s32[]{:T(128)}, f32[4,2,128,768]{3,2,1,0:T(8,128)}, f32[4,2,128,768]{3,2,1,0:T(8,128)}, f32[4,2,128]{2,1,0:T(2,128)S(1)}, bf16[4,2,128,768]{3,2,1,0...) while((s32[]{:T(128)}, f32[4,2,128,768]{3,2,1,0:T(8,128)}, ...), condition=%wide.region_5.6_spmd.clone, body=%wide.region_4.5_spmd.clone.sunk | while | flops 151257344 | bytes 3349329 | solution.py:85
  70.8 1.3 fusion.52
  72.1 1.2 fusion.54
  73.3 2.1 %fusion.53 = f32[4,2,128,768]{3,2,1,0:T(8,128)} fusion(f32[4,2,128,768]{3,2,1,0:T(8,128)} %get-tuple-element.128, s32[]{:T(128)} %get-tuple-element.127, bf16[2,128,128]{2,1,0:T(8,128)(2,1)S(1)} %fusion.52, bf16[4,2,128,768]{3,2,1,0:T(8,128)(2,1)} %get-tuple-element.139), kind=kOutput, calls=%fused_computation.8.clone.1 | convolution fusion | flops 50331648 | bytes 1246208 | tf_op jit(solution)/shard_map/while/body/eval_jaxpr/bsl,bld->bsd/dot_general | solution.py:81
  75.4 1.3 fusion.52
  76.7 1.2 fusion.54
  77.9 2.1 %fusion.53 = f32[4,2,128,768]{3,2,1,0:T(8,128)} fusion(f32[4,2,128,768]{3,2,1,0:T(8,128)} %get-tuple-element.128, s32[]{:T(128)} %get-tuple-element.127, bf16[2,128,128]{2,1,0:T(8,128)(2,1)S(1)} %fusion.52, bf16[4,2,128,768]{3,2,1,0:T(8,128)(2,1)} %get-tuple-element.139), kind=kOutput, calls=%fused_computation.8.clone.1 | convolution fusion | flops 50331648 | bytes 1246208 | tf_op jit(solution)/shard_map/while/body/eval_jaxpr/bsl,bld->bsd/dot_general | solution.py:81
  80.0 1.3 fusion.52
  81.3 1.2 fusion.54
  82.5 2.1 %fusion.53 = f32[4,2,128,768]{3,2,1,0:T(8,128)} fusion(f32[4,2,128,768]{3,2,1,0:T(8,128)} %get-tuple-element.128, s32[]{:T(128)} %get-tuple-element.127, bf16[2,128,128]{2,1,0:T(8,128)(2,1)S(1)} %fusion.52, bf16[4,2,128,768]{3,2,1,0:T(8,128)(2,1)} %get-tuple-element.139), kind=kOutput, calls=%fused_computation.8.clone.1 | convolution fusion | flops 50331648 | bytes 1246208 | tf_op jit(solution)/shard_map/while/body/eval_jaxpr/bsl,bld->bsd/dot_general | solution.py:81
  84.7 1.3 fusion.52
  86.0 1.2 fusion.54
  87.2 2.1 %fusion.53 = f32[4,2,128,768]{3,2,1,0:T(8,128)} fusion(f32[4,2,128,768]{3,2,1,0:T(8,128)} %get-tuple-element.128, s32[]{:T(128)} %get-tuple-element.127, bf16[2,128,128]{2,1,0:T(8,128)(2,1)S(1)} %fusion.52, bf16[4,2,128,768]{3,2,1,0:T(8,128)(2,1)} %get-tuple-element.139), kind=kOutput, calls=%fused_computation.8.clone.1 | convolution fusion | flops 50331648 | bytes 1246208 | tf_op jit(solution)/shard_map/while/body/eval_jaxpr/bsl,bld->bsd/dot_general | solution.py:81
  89.3 1.9 copy-done.1
  91.2 3.5 %copy.35 = f32[1,8,128,768]{3,1,0,2:T(8,128)} copy(f32[1,8,128,768]{3,2,1,0:T(8,128)S(1)} %bitcast.91) | data formatting | bytes 6291456 | tf_op jit(solution)/shard_map/broadcast_in_dim;reshape | solution.py:20
  94.7 9.1 %all-to-all-start.2 = ((f32[1,8,128,768]{3,1,0,2:T(8,128)}), f32[1,8,128,768]{3,1,0,2:T(8,128)S(1)}, u32[]{:S(2)}, u32[]{:S(2)}) async-start(f32[1,8,128,768]{3,1,0,2:T(8,128)} %copy.35), calls=%async_computation.2 | async-start | bytes 6291456 | tf_op jit(solution)/shard_map/all_to_all | solution.py:20
  103.8 33.4 %reduce-scatter.2.cloned.1.call-done = f32[512,768]{1,0:T(8,128)} async-done(((f32[1024,768]{1,0:T(8,128)}), f32[512,768]{1,0:T(8,128)}) %reduce-scatter.2.cloned.1.call-update) | async-done | bytes 1572880 | tf_op jit(solution)/shard_map/reduce_scatter | solution.py:27
  137.2 5.5 %bitcast_subtract_fusion = (f32[512,768]{1,0:T(8,128)}, f32[1,512,768]{2,1,0:T(8,128)}, f32[1,512,768]{2,1,0:T(8,128)}) fusion(bf16[1024,768]{1,0:T(8,128)(2,1)} %bitcast.90, s32[]{:T(128)S(6)} %select_n.41, f32[512,768]{1,0:T(8,128)} %reduce-scatter.2.cloned.1.call-done, f32[1,512,768]{2,1,0:T(8,128)} %param.12, f32[1,512,768]{2,1,0:T(8,128)} %param.13), kind=kLoop, calls=%fused_computation.36 | loop fusion | flops 5505024 | bytes 10223620 | tf_op jit(solution)/shard_map/sub | solution.py:37
  142.7 20.4 %all-to-all-done.2 = f32[1,8,128,768]{3,1,0,2:T(8,128)S(1)} async-done(((f32[1,8,128,768]{3,1,0,2:T(8,128)}), f32[1,8,128,768]{3,1,0,2:T(8,128)S(1)}, u32[]{:S(2)}, u32[]{:S(2)}) %all-to-all-start.2) | async-done | bytes 3145760 | tf_op jit(solution)/shard_map/all_to_all | solution.py:20
  163.1 1.0 copy.37
  164.1 0.3 copy.33
  164.5 5.2 %gather_fusion.2 = f32[1024,768]{1,0:T(8,128)} fusion(f32[1024,768]{1,0:T(8,128)S(1)} %bitcast.84, s32[1024]{0:T(1024)S(1)} %broadcast_clamp_fusion), kind=kCustom, calls=%fused_computation.2 | custom fusion | bytes 6295552 | tf_op jit(solution)/shard_map/gather | solution.py:22
  169.7 3.4 %bitcast_reduce_fusion = f32[128,768]{1,0:T(8,128)} fusion(f32[1024,768]{1,0:T(8,128)} %gather_fusion.2), kind=kLoop, calls=%fused_computation.31 | loop fusion | flops 688128 | bytes 3538944 | tf_op jit(solution)/shard_map/reduce_sum | solution.py:23
  173.1 14.7 %all-gather.2.cloned.1.call-done = f32[1024,768]{1,0:T(8,128)} async-done(((f32[512,768]{1,0:T(8,128)}), f32[1024,768]{1,0:T(8,128)}) %all-gather.2.cloned.1.call-update) | async-done | bytes 3145744 | tf_op jit(solution)/shard_map/all_gather | solution.py:38
  187.8 3.8 %copy.50 = f32[1024,768]{1,0:T(8,128)} copy(f32[1024,768]{1,0:T(8,128)} %all-gather.2.cloned.1.call-done) | data formatting | bytes 6291456
  (27 shorter events, 0.4 us)
Async XLA Ops:
  7.2 20.1 %copy-start = (bf16[128,768]{1,0:T(8,128)(2,1)S(1)}, bf16[128,768]{1,0:T(8,128)(2,1)}, u32[]{:S(2)}) copy-start(bf16[128,768]{1,0:T(8,128)(2,1)} %param.8) | copy-start | bytes 589828
  9.0 5.3 %copy-start.2 = (s32[128,8]{0,1:T(8,128)S(1)}, s32[128,8]{0,1:T(8,128)}, u32[]{:S(2)}) copy-start(s32[128,8]{0,1:T(8,128)} %param.10) | copy-start | bytes 12292
  19.8 14.0 %all-to-all-start = ((bf16[16,8,8]{2,1,0:T(8,128)(2,1)}), bf16[16,8,8]{2,1,0:T(8,128)(2,1)S(1)}, u32[]{:S(2)}, u32[]{:S(2)}) async-start(bf16[16,8,8]{2,1,0:T(8,128)(2,1)} %reshape.108), calls=%async_computation | async-start | bytes 65536 | tf_op jit(solution)/shard_map/all_to_all | solution.py:64
  33.8 36.8 %all-to-all-start.1 = ((bf16[16,8,8,768]{3,2,1,0:T(8,128)(2,1)}), bf16[16,8,8,768]{3,2,1,0:T(8,128)(2,1)S(1)}, u32[]{:S(2)}, u32[]{:S(2)}) async-start(bf16[16,8,8,768]{3,2,1,0:T(8,128)(2,1)} %broadcast_select_fusion), calls=%async_computation.1 | async-start | bytes 3145728 | tf_op jit(solution)/shard_map/all_to_all | solution.py:63
  38.7 98.6 %reduce-scatter.2.cloned.1.call-start = ((), (), s32[]{:S(2)}) async-start(), calls=%async_computation.4 | async-start | bytes 4718592 | tf_op jit(solution)/shard_map/reduce_scatter | solution.py:27
  89.3 1.9 copy-start.1
  94.7 68.5 %all-to-all-start.2 = ((f32[1,8,128,768]{3,1,0,2:T(8,128)}), f32[1,8,128,768]{3,1,0,2:T(8,128)S(1)}, u32[]{:S(2)}, u32[]{:S(2)}) async-start(f32[1,8,128,768]{3,1,0,2:T(8,128)} %copy.35), calls=%async_computation.2 | async-start | bytes 6291456 | tf_op jit(solution)/shard_map/all_to_all | solution.py:20
  103.8 84.1 %all-gather.2.cloned.1.call-start = ((), (), s32[]{:S(2)}) async-start(), calls=%async_computation.5 | async-start | bytes 4718592 | tf_op jit(solution)/shard_map/all_gather | solution.py:38
Sparse Core Ops, SparseCore 0:
  89.4 47.7 reduce-scatter.1
  142.8 44.9 all-gather.1
where the time goes:
time: 199 us; the launch traced here: 198 us
  waiting for transfers between devices  101 us (51%)
  local copies, waits for them, and re-layouts  31.2 us (16%)
  starting transfers between devices  21.4 us (11%)
  matrix products  18.5 us (9%)
  between operations  14.3 us (7%)
  other arithmetic  11.6 us (6%)
    reduce_scatter x1, waiting for transfers between devices, update_shard(): lax.psum_scatter(weight_grad, 'rep', scatter_dimension=0, tiled=True)  33.4 us
    all_to_all x1, waiting for transfers between devices, body(): lax.all_to_all(send_rows, 'lab', split_axis=0, concat_axis=2, tiled=True)  31.8 us
    all_to_all x1, waiting for transfers between devices, send_back(): lax.all_to_all(row_parts[None], 'lab', split_axis=2, concat_axis=0, tiled...  20.4 us
    all_gather x1, waiting for transfers between devices, update_shard(): new_weight = lax.all_gather(fresh_rows, 'rep', axis=0, tiled=True)  14.7 us
    all_to_all x1, starting transfers between devices, send_back(): lax.all_to_all(row_parts[None], 'lab', split_axis=2, concat_axis=0, tiled...  9.09 us
    dot_general x4, matrix products, tile_work(): jnp.einsum('bsl,bld->bsd', slopes, tiles, preferred_element_type=jnp.floa...  8.51 us
    all_to_all x1, starting transfers between devices, body(): lax.all_to_all(send_marks, 'lab', split_axis=0, concat_axis=2, tiled=True)  7.36 us
    unnamed x9, local copies, waits for them, and re-layouts  6.56 us
  transfers between devices with their start and end apart: 5, of which 5 were waited for; matrix products, arithmetic and copies ran while one was open for 12% of the time, Pallas kernels for 0%

commit v1 on v0

v1 whole, which is shorter than its diff:
```python
import functools

import jax
import jax.numpy as jnp
from jax import lax
from jax.experimental import pallas as pl
from jax.experimental.pallas import tpu as pltpu
from jax.sharding import PartitionSpec as P

BLOCK = 128
F32 = jnp.float32
BF16 = jnp.bfloat16
MESH = pl.DeviceIdType.MESH

beta_first = 0.9
beta_second = 0.999
learn_rate = 0.01
adam_epsilon = 1e-08
step_count = 100.0


def chip_at(place, chips):
    place = lax.rem(place + 2 * chips, chips)
    back = lax.div(place, chips // 2)
    return 2 * place + back * (2 * (chips - 1 - place) + 1 - 2 * place)


def kernel(
    reps, labs, rows, depth, names, local, shard,
    q_ref, info_ref, w_ref, first_ref, second_ref,
    grad_ref, step_ref, sum_ref,
    qbuf, ibuf, wg, slope, own_part, pair_out, pair_in, ring_out, ring_in,
    wg_out, wg_in, first, second,
    gather_send, gather_recv, note_send, note_recv,
    twin_send, twin_recv, twin_note_send, twin_note_recv,
    part_send, part_recv, ring_send, ring_recv,
    wg_send, wg_recv, step_send, step_recv, load_sem,
):
    chips = labs // 2
    turns = chips // 2
    half = rows // 2
    tile = min(shard, 256)
    piece = min(shard, BLOCK)
    pieces = shard // piece
    rep = lax.axis_index("rep")
    lab = lax.axis_index("lab")
    core = lax.rem(lab, 2)
    chip = lax.div(lab, 2)
    odd = lax.rem(chip, 2)
    rank = lax.div(chip, 2)
    place = rank + odd * (chips - 1 - 2 * rank)
    ahead = (rep, chip_at(place + 1, chips) * 2 + core)
    behind = (rep, chip_at(place - 1, chips) * 2 + core)
    twin = (rep, chip * 2 + 1 - core)
    partners = [(lax.rem(rep + j, reps), lab) for j in range(1, reps)]

    load_first = pltpu.make_async_copy(first_ref, first, load_sem.at[0])
    load_second = pltpu.make_async_copy(second_ref, second, load_sem.at[1])
    load_first.start()
    load_second.start()

    barrier = pltpu.get_barrier_semaphore()
    everyone = [ahead, behind, twin] + partners
    for other in everyone:
        pl.semaphore_signal(barrier, inc=1, device_id=other, device_id_type=MESH)
    qbuf[0:rows, :] = q_ref[...]
    ibuf[0] = info_ref[...]
    pl.semaphore_wait(barrier, len(everyone))

    def remote(src, dst, send, recv, index, device):
        copy = pltpu.make_async_remote_copy(
            src_ref=src, dst_ref=dst, send_sem=send.at[index], recv_sem=recv.at[index],
            device_id=device, device_id_type=MESH,
        )
        copy.start()
        return copy

    def chunk(way, turn):
        if turn == 0:
            return 0
        if turn == turns:
            return 2 + 4 * (turns - 1)
        return 2 + 4 * (turn - 1) + 2 * way

    def sem(way, turn):
        return 2 * turn - 1 + way if turn else 0

    def span(way, turn):
        if turn == turns:
            return (half * way, half)
        return (0, rows)

    gathers, twins, pending = {}, {}, []

    def send_on(way, turn):
        low, count = span(way, turn)
        src, dst = chunk(way, turn - 1), chunk(way, turn)
        k = sem(way, turn)
        device = ahead if way == 0 else behind
        got = [
            remote(
                qbuf.at[pl.ds(src * rows + low, count)], qbuf.at[pl.ds(dst * rows + low, count)],
                gather_send, gather_recv, k, device,
            )
        ]
        if turn < turns or way == 0:
            got.append(remote(ibuf.at[src], ibuf.at[dst], note_send, note_recv, k, device))
        gathers[way, turn] = got

    def send_twin(way, turn):
        low, count = span(way, turn)
        c = chunk(way, turn)
        k = sem(way, turn)
        got = [
            remote(
                qbuf.at[pl.ds(c * rows + low, count)], qbuf.at[pl.ds((c + 1) * rows + low, count)],
                twin_send, twin_recv, k, twin,
            )
        ]
        if turn < turns or way == 0:
            got.append(remote(ibuf.at[c], ibuf.at[c + 1], twin_note_send, twin_note_recv, k, twin))
        twins[way, turn] = got

    def one_tile(group, start):
        low = chunk(0, group)
        count = 2 if group in (0, turns) else 4
        width = count * rows
        queries = qbuf[low * rows : low * rows + width, :]
        listed = jnp.concatenate([ibuf[low + i, 0:names, :] for i in range(count)], axis=1).astype(F32)
        wanted = jnp.concatenate(
            [ibuf[low + i, names : 2 * names, :] for i in range(count)], axis=1
        ).astype(F32)
        logits = lax.dot_general(
            w_ref[pl.ds(start, tile), :], queries, (((1,), (1,)), ((), ())),
            preferred_element_type=F32,
        )
        parts = []
        for c in range(tile // piece):
            label = lab * local + start + c * piece
            block = lax.div(label, BLOCK)
            shift = lax.rem(label, BLOCK).astype(F32)
            mark = jnp.sum(
                jnp.where(listed == block.astype(F32), wanted + 1.0, 0.0), axis=0, keepdims=True
            )
            offsets = lax.broadcasted_iota(jnp.int32, (piece, width), 0).astype(F32) + 1.0
            target = (offsets == mark - shift).astype(F32)
            value = jax.nn.sigmoid(logits[c * piece : (c + 1) * piece, :]) - target
            parts.append(jnp.where(mark > 0.0, value, 0.0).astype(BF16))
        slopes = parts[0] if len(parts) == 1 else jnp.concatenate(parts, axis=0)
        slope[pl.ds(start, tile), 0:width] = slopes
        term = jnp.dot(slopes, queries, preferred_element_type=F32)
        if group == 0:
            wg[pl.ds(start, tile), :] = term
        else:
            wg[pl.ds(start, tile), :] = wg[pl.ds(start, tile), :] + term

    per_shard = shard // tile

    def tile_start(j):
        owner = lax.rem(rep + 1 + lax.div(j, per_shard), reps)
        return pl.multiple_of(owner * shard + lax.rem(j, per_shard) * tile, tile)

    def pair_of(way, turn):
        return chunk(way, turn) // 2

    part_copies = {}

    def row_parts(group):
        ways = (0,) if group in (0, turns) else (0, 1)
        for way in ways:
            i = pair_of(way, group)
            lanes = way * 2 * rows
            part = lax.dot_general(
                slope[:, lanes : lanes + 2 * rows], w_ref[...], (((0,), (0,)), ((), ())),
                preferred_element_type=F32,
            )
            own_part[i] = part[0:rows]
            pair_out[i] = part[rows : 2 * rows].astype(BF16)
            part_copies[i] = remote(
                pair_out.at[i], pair_in.at[i], part_send, part_recv, i, twin
            )

    def wait_twins(group):
        ways = (0,) if group == 0 else (0, 1)
        for way in ways:
            for copy in twins[way, group]:
                copy.wait_recv()

    send_on(0, 1)
    send_on(1, 1)
    send_twin(0, 0)
    for turn in range(1, turns + 1):
        for way in (0, 1):
            for copy in gathers[way, turn]:
                copy.wait_recv()
        for way in (0, 1):
            if turn < turns:
                send_on(way, turn + 1)
            send_twin(way, turn)
        group = turn - 1
        wait_twins(group)

        @pl.loop(0, local // tile)
        def _(j):
            one_tile(group, tile_start(j))

        row_parts(group)
    wait_twins(turns)

    wg_copies = {}
    for j in range(local // tile):
        start = tile_start(j)
        one_tile(turns, start)
        peer = j // per_shard
        if peer < reps - 1:
            low = (j % per_shard) * tile
            wg_out[peer, low : low + tile, :] = wg[pl.ds(start, tile), :].astype(BF16)
            for y in range(low // piece, (low + tile) // piece):
                wg_copies[peer, y] = remote(
                    wg_out.at[peer, pl.ds(y * piece, piece)],
                    wg_in.at[peer, pl.ds(y * piece, piece)],
                    wg_send, wg_recv, peer * pieces + y, partners[peer],
                )
    row_parts(turns)
    load_first.wait()
    load_second.wait()

    ring_copies = {}

    def ring_step(s):
        for way in (0, 1):
            i = pair_of(1 - way, turns - s)
            if s > 0 or way == 0:
                part_copies[i].wait_recv()
            k = way * turns + s
            device = ahead if way == 0 else behind
            if s == 0:
                low = half * way
                value = own_part[i, low : low + half, :] + pair_in[i, low : low + half, :].astype(F32)
                ring_out[k, 0:half, :] = value.astype(BF16)
                ring_copies[way, s] = remote(
                    ring_out.at[k, pl.ds(0, half)], ring_in.at[k, pl.ds(0, half)],
                    ring_send, ring_recv, k, device,
                )
                continue
            ring_copies[way, s - 1].wait_recv()
            value = own_part[i] + pair_in[i].astype(F32)
            if s == 1:
                low = half * way
                came = ring_in[k - 1, 0:half, :].astype(F32)
                mixed = [value[0:half], value[half:rows]]
                mixed[way] = mixed[way] + came
                ring_out[k, 0:half, :] = mixed[0].astype(BF16)
                ring_out[k, half:rows, :] = mixed[1].astype(BF16)
            else:
                ring_out[k] = (value + ring_in[k - 1].astype(F32)).astype(BF16)
            ring_copies[way, s] = remote(
                ring_out.at[k], ring_in.at[k], ring_send, ring_recv, k, device
            )

    def ring_end():
        part_copies[0].wait_recv()
        value = own_part[0] + pair_in[0].astype(F32)
        for way in (0, 1):
            ring_copies[way, turns - 1].wait_recv()
            value = value + ring_in[way * turns + turns - 1].astype(F32)
        grad_ref[...] = value

    step_copies = []

    def adam(y):
        low = y * piece
        here = pl.multiple_of(rep * shard + low, piece)
        total = wg[pl.ds(here, piece), :]
        for peer in range(reps - 1):
            wg_copies[peer, y].wait_recv()
            total = total + wg_in[peer, low : low + piece, :].astype(F32)
        sum_ref[low : low + piece, :] = total
        new_first = beta_first * first[low : low + piece, :] + (1.0 - beta_first) * total
        new_second = beta_second * second[low : low + piece, :] + (1.0 - beta_second) * total * total
        first_hat = new_first * (1.0 / (1.0 - beta_first**step_count))
        second_hat = new_second * (1.0 / (1.0 - beta_second**step_count))
        step_ref[pl.ds(here, piece), :] = (
            first_hat / (jnp.sqrt(second_hat) + adam_epsilon)
        ).astype(BF16)
        for peer in range(reps - 1):
            step_copies.append(
                remote(
                    step_ref.at[pl.ds(here, piece)], step_ref.at[pl.ds(here, piece)],
                    step_send, step_recv, peer * pieces + y, partners[peer],
                )
            )

    ring_step(0)
    ring_step(1)
    for k in range(max(pieces, turns - 1)):
        if k < pieces:
            adam(k)
        if k + 2 < turns:
            ring_step(k + 2)
        if k + 2 == turns:
            ring_end()

    for copies in (gathers, twins):
        for group in copies.values():
            for copy in group:
                copy.wait_send()
    for copies in (part_copies, ring_copies, wg_copies):
        for copy in copies.values():
            copy.wait_send()
    for copy in step_copies:
        copy.wait_send()
        copy.wait_recv()


def body(reps, labs, queries, shortlist, positive, label_weight, first_moment, second_moment):
    rows, depth = queries.shape
    names = shortlist.shape[1]
    local = label_weight.shape[0]
    shard = first_moment.shape[1]
    chips = labs // 2
    turns = chips // 2
    tile = min(shard, 256)
    piece = min(shard, BLOCK)
    pieces = shard // piece
    info = jnp.concatenate([shortlist.T, positive.T], axis=0).astype(BF16)
    vmem = pl.BlockSpec(memory_space=pltpu.VMEM)
    anywhere = pl.BlockSpec(memory_space=pl.ANY)
    dma = pltpu.SemaphoreType.DMA
    scratch = [
        pltpu.VMEM((labs * rows, depth), BF16),
        pltpu.VMEM((labs, 2 * names, rows), BF16),
        pltpu.VMEM((local, depth), F32),
        pltpu.VMEM((local, 4 * rows), BF16),
        pltpu.VMEM((chips, rows, depth), F32),
        pltpu.VMEM((chips, rows, depth), BF16),
        pltpu.VMEM((chips, rows, depth), BF16),
        pltpu.VMEM((2 * turns, rows, depth), BF16),
        pltpu.VMEM((2 * turns, rows, depth), BF16),
        pltpu.VMEM((reps - 1, shard, depth), BF16),
        pltpu.VMEM((reps - 1, shard, depth), BF16),
        pltpu.VMEM((shard, depth), F32),
        pltpu.VMEM((shard, depth), F32),
    ]
    scratch += [dma((2 * turns + 1,))] * 8
    scratch += [dma((chips,))] * 2 + [dma((2 * turns,))] * 2
    scratch += [dma(((reps - 1) * pieces,))] * 4 + [dma((2,))]
    grad, step, total = pl.pallas_call(
        functools.partial(kernel, reps, labs, rows, depth, names, local, shard),
        out_shape=(
            jax.ShapeDtypeStruct((rows, depth), F32),
            jax.ShapeDtypeStruct((local, depth), BF16),
            jax.ShapeDtypeStruct((shard, depth), F32),
        ),
        in_specs=[vmem, vmem, vmem, anywhere, anywhere],
        out_specs=(vmem, vmem, vmem),
        scratch_shapes=scratch,
        compiler_params=pltpu.CompilerParams(
            collective_id=0, has_side_effects=True, vmem_limit_bytes=56 * 1024 * 1024
        ),
    )(queries, info, label_weight, first_moment[0], second_moment[0])
    total = total[None]
    new_first = beta_first * first_moment + (1.0 - beta_first) * total
    new_second = beta_second * second_moment + (1.0 - beta_second) * total * total
    new_weight = label_weight.astype(F32) - learn_rate * step.astype(F32)
    return (grad, new_weight, new_first, new_second)


def solution(mesh):
    in_specs = (
        P(("rep", "lab"), None),
        P(("rep", "lab"), None),
        P(("rep", "lab"), None),
        P("lab", None),
        P("rep", "lab", None),
        P("rep", "lab", None),
    )
    out_specs = (
        P(("rep", "lab"), None),
        P("lab", None),
        P("rep", "lab", None),
        P("rep", "lab", None),
    )
    run = functools.partial(body, mesh.shape["rep"], mesh.shape["lab"])
    return jax.shard_map(run, mesh=mesh, in_specs=in_specs, out_specs=out_specs, check_vma=False)
```

time: 199 us -> 76.6 us (0.38)
  waiting for transfers between devices: 101 us -> 0 us
  Pallas kernels: 0 us -> 67.9 us
  local copies, waits for them, and re-layouts: 31.2 us -> 0.77 us
  starting transfers between devices: 21.4 us -> 0 us
  matrix products: 18.5 us -> 0 us
  between operations: 14.3 us -> 0.69 us
  other arithmetic: 11.6 us -> 7.05 us
    pallas_call x0 -> x1, Pallas kernels: none -> 67.9 us  [body(): pl.pallas_call(functools.partial(kernel, reps, labs, rows, depth, names,...]
    all_to_all x3 -> x0, waiting for transfers between devices: 53.3 us -> none  [the longest x1 31.8 us: body(): lax.all_to_all(send_rows, 'lab', split_axis=0, concat_axis=2, tiled=True)]
    reduce_scatter x1 -> x0, waiting for transfers between devices: 33.4 us -> none  [update_shard(): lax.psum_scatter(weight_grad, 'rep', scatter_dimension=0, tiled=True)]
    all_to_all x3 -> x0, starting transfers between devices: 21.3 us -> none  [the longest x1 9.09 us: send_back(): lax.all_to_all(row_parts[None], 'lab', split_axis=2, concat_axis=0, tiled...]
    dot_general x12 -> x0, matrix products: 18.5 us -> none  [the longest x4 8.51 us: tile_work(): jnp.einsum('bsl,bld->bsd', slopes, tiles, preferred_element_type=jnp.floa...]
    all_gather x1 -> x0, waiting for transfers between devices: 14.7 us -> none  [update_shard(): new_weight = lax.all_gather(fresh_rows, 'rep', axis=0, tiled=True)]
    gather x3 -> x0, local copies, waits for them, and re-layouts: 13.8 us -> none  [the longest x1 5.23 us: send_back(): pieces = flat_back[target_slot].reshape(rows_here, K, D)]
    unnamed x9 -> x11, local copies, waits for them, and re-layouts: 6.56 us -> 0.77 us
  transfers between devices with their start and end apart: 5 -> 0, of which waited for: 5 -> 0; matrix products, arithmetic and copies ran while one was open for 12% -> 0% of each run, Pallas kernels for 0% -> 0%
where the time goes in v1:
time: 76.6 us; the launch traced here: 76.4 us
  Pallas kernels  67.9 us (89%)
  other arithmetic  7.05 us (9%)
  local copies, waits for them, and re-layouts  0.77 us (1%)
    pallas_call x1, Pallas kernels, body(): pl.pallas_call(functools.partial(kernel, reps, labs, rows, depth, names,...  67.9 us
    sub x1, other arithmetic, body(): new_weight = label_weight.astype(F32) - learn_rate * step.astype(F32)  3.63 us
    add x1, other arithmetic, body(): beta_second * second_moment + (1.0 - beta_second) * total * total  2.12 us

profile of v1, /device:TPU:0, one launch (start us, length us, event | category | flops | bytes accessed | tf_op | source)
XLA Modules:
  0.0 76.4 jit_solution(18225196020829300766)
XLA Ops:
  0.6 0.7 convert_bitcast_fusion
  1.3 0.6 pad_maximum_fusion.info_ref
  1.9 0.0 copy-start
  1.9 67.9 %shard_map.93 = (f32[128,768]{1,0:T(8,128)}, bf16[1024,768]{1,0:T(8,128)(2,1)}, f32[512,768]{1,0:T(8,128)}) custom-call(bf16[128,768]{1,0:T(8,128)(2,1)} %q_ref.1, bf16[16,128]{1,0:T(8,128)(2,1)} %pad_maximum_fusion.info_ref, bf16[1024,768]{1,0:T(8,128)(2,1)} %w_ref.1, f32[512,768]{1,0:T(8,128)} %bitcast.12, f32[512,768]{1,0:T(8,128)} %bitcast.13), custom_call_target="tpu_custom_call" | custom-call | tf_op jit(solution)/shard_map/pallas_call | solution.py:348
  69.8 0.0 copy-done
  69.8 0.0 copy-start.1
  69.8 0.0 copy-start.2
  69.8 0.0 copy-start.3
  69.8 3.6 %multiply_subtract_fusion = f32[1024,768]{1,0:T(8,128)} fusion(bf16[1024,768]{1,0:T(8,128)(2,1)} %get-tuple-element.8, bf16[1024,768]{1,0:T(8,128)(2,1)S(1)} %copy-done), kind=kLoop, calls=%fused_computation | loop fusion | flops 3145728 | bytes 6291456 | tf_op jit(solution)/shard_map/sub | solution.py:365
  73.5 0.0 copy-done.1
  73.5 0.0 copy-done.2
  73.5 0.0 copy-done.3
  73.5 0.0 copy-start.4
  73.5 2.1 %fusion.1 = (f32[1,512,768]{2,1,0:T(8,128)}, f32[1,512,768]{2,1,0:T(8,128)}) fusion(f32[512,768]{1,0:T(8,128)S(1)} %copy-done.3, f32[1,512,768]{2,1,0:T(8,128)S(1)} %copy-done.2, f32[1,512,768]{2,1,0:T(8,128)S(1)} %copy-done.1), kind=kLoop, calls=%fused_computation.3 | loop fusion | flops 2752512 | bytes 7864320 | tf_op jit(solution)/shard_map/add | solution.py:364
  75.6 0.0 copy-done.4
  75.6 0.7 copy.11
Async XLA Ops:
  1.9 67.9 %copy-start = (bf16[1024,768]{1,0:T(8,128)(2,1)S(1)}, bf16[1024,768]{1,0:T(8,128)(2,1)}, u32[]{:S(2)}) copy-start(bf16[1024,768]{1,0:T(8,128)(2,1)} %w_ref.1) | copy-start | bytes 4718596
  69.8 3.7 %copy-start.1 = (f32[1,512,768]{2,1,0:T(8,128)S(1)}, f32[1,512,768]{2,1,0:T(8,128)}, u32[]{:S(2)}) copy-start(f32[1,512,768]{2,1,0:T(8,128)} %param.10) | copy-start | bytes 4718596
  69.8 3.7 %copy-start.2 = (f32[1,512,768]{2,1,0:T(8,128)S(1)}, f32[1,512,768]{2,1,0:T(8,128)}, u32[]{:S(2)}) copy-start(f32[1,512,768]{2,1,0:T(8,128)} %param.11) | copy-start | bytes 4718596
  69.8 3.6 %copy-start.3 = (f32[512,768]{1,0:T(8,128)S(1)}, f32[512,768]{1,0:T(8,128)}, u32[]{:S(2)}) copy-start(f32[512,768]{1,0:T(8,128)} %get-tuple-element.9) | copy-start | bytes 4718596
  73.5 2.1 %copy-start.4 = (f32[128,768]{1,0:T(8,128)S(1)}, f32[128,768]{1,0:T(8,128)}, u32[]{:S(2)}) copy-start(f32[128,768]{1,0:T(8,128)} %get-tuple-element.18) | copy-start | bytes 1179652

commit v2 on v1

v2 whole, which is shorter than its diff:
```python
import functools

import jax
import jax.numpy as jnp
from jax import lax
from jax.experimental import pallas as pl
from jax.experimental.pallas import tpu as pltpu
from jax.sharding import PartitionSpec as P

BLOCK = 128
CAP = 8
F32 = jnp.float32
BF16 = jnp.bfloat16
MESH = pl.DeviceIdType.MESH

beta_first = 0.9
beta_second = 0.999
learn_rate = 0.01
adam_epsilon = 1e-08
step_count = 100.0


def chip_at(place, chips):
    place = lax.rem(place + 2 * chips, chips)
    back = lax.div(place, chips // 2)
    return 2 * place + back * (2 * (chips - 1 - place) + 1 - 2 * place)


def kernel(
    reps, labs, rows, depth, names, local, shard,
    q_ref, info_ref, w_ref, first_ref, second_ref,
    grad_ref, step_ref, sum_ref,
    qbuf, ibuf, wg, gbuf, mbuf, pbuf, qslot, earlier, own_part, pair_out, pair_in,
    ring_out, ring_in, last_out, last_in, wg_out, wg_in, first, second,
    gather_send, gather_recv, note_send, note_recv,
    twin_send, twin_recv, twin_note_send, twin_note_recv,
    part_send, part_recv, ring_send, ring_recv,
    wg_send, wg_recv, step_send, step_recv, load_sem,
):
    chips = labs // 2
    turns = chips // 2
    half = rows // 2
    blocks = local // BLOCK
    piece = min(shard, BLOCK)
    pieces = shard // piece
    rep = lax.axis_index("rep")
    lab = lax.axis_index("lab")
    core = lax.rem(lab, 2)
    chip = lax.div(lab, 2)
    odd = lax.rem(chip, 2)
    rank = lax.div(chip, 2)
    place = rank + odd * (chips - 1 - 2 * rank)
    ahead = (rep, chip_at(place + 1, chips) * 2 + core)
    behind = (rep, chip_at(place - 1, chips) * 2 + core)
    twin = (rep, chip * 2 + 1 - core)
    partners = [(lax.rem(rep + j, reps), lab) for j in range(1, reps)]

    load_first = pltpu.make_async_copy(first_ref, first, load_sem.at[0])
    load_second = pltpu.make_async_copy(second_ref, second, load_sem.at[1])
    load_first.start()
    load_second.start()

    barrier = pltpu.get_barrier_semaphore()
    everyone = [ahead, behind, twin] + partners
    for other in everyone:
        pl.semaphore_signal(barrier, inc=1, device_id=other, device_id_type=MESH)
    qbuf[0:rows, :] = q_ref[...]
    ibuf[0] = info_ref[...]
    pl.semaphore_wait(barrier, len(everyone))

    def remote(src, dst, send, recv, index, device):
        copy = pltpu.make_async_remote_copy(
            src_ref=src, dst_ref=dst, send_sem=send.at[index], recv_sem=recv.at[index],
            device_id=device, device_id_type=MESH,
        )
        copy.start()
        return copy

    def chunk(way, turn):
        if turn == 0:
            return 0
        if turn == turns:
            return 2 + 4 * (turns - 1)
        return 2 + 4 * (turn - 1) + 2 * way

    def sem(way, turn):
        return 2 * turn - 1 + way if turn else 0

    gathers, twins = {}, {}
    slots = 2 * CAP

    def halves(way, turn):
        return (way,) if turn == turns else (0, 1)

    def send_on(way, turn, part):
        src, dst = chunk(way, turn - 1), chunk(way, turn)
        k = 2 * sem(way, turn) + part
        device = ahead if way == 0 else behind
        low = part * half
        got = [
            remote(
                qbuf.at[pl.ds(src * rows + low, half)], qbuf.at[pl.ds(dst * rows + low, half)],
                gather_send, gather_recv, k, device,
            )
        ]
        if part == 0:
            got.append(remote(ibuf.at[src], ibuf.at[dst], note_send, note_recv, k, device))
        gathers[way, turn, part] = got

    def send_twin(way, turn, part):
        c = chunk(way, turn)
        k = 2 * sem(way, turn) + part
        low = part * half
        got = [
            remote(
                qbuf.at[pl.ds(c * rows + low, half)], qbuf.at[pl.ds((c + 1) * rows + low, half)],
                twin_send, twin_recv, k, twin,
            )
        ]
        if part == 0:
            got.append(remote(ibuf.at[c], ibuf.at[c + 1], twin_note_send, twin_note_recv, k, twin))
        twins[way, turn, part] = got

    def pair_of(way, turn):
        return chunk(way, turn) // 2

    def pick(i):
        width = 2 * rows
        pair = (2 * i, 2 * i + 1)
        listed = jnp.concatenate([ibuf[c, 0:names, :] for c in pair], axis=1).astype(F32)
        wanted = jnp.concatenate([ibuf[c, names : 2 * names, :] for c in pair], axis=1).astype(F32)
        hits, marks = [], []
        for b in range(blocks):
            same = listed == (lab * blocks + b).astype(F32)
            hits.append(jnp.sum(jnp.where(same, 1.0, 0.0), axis=0, keepdims=True))
            marks.append(jnp.sum(jnp.where(same, wanted + 1.0, 0.0), axis=0, keepdims=True))
        hit = jnp.concatenate(hits, axis=0)
        later = lax.broadcasted_iota(jnp.int32, (blocks, width), 1) >= rows
        order = jnp.dot(hit.astype(BF16), earlier[...], preferred_element_type=F32)
        order = order + jnp.where(later, float(CAP), 0.0)
        order = jnp.where(hit > 0.0, order, -1.0)
        number = lax.broadcasted_iota(jnp.int32, (slots, width), 0).astype(F32)
        chosen = []
        for b in range(blocks):
            mine = number == order[b : b + 1, :]
            mark = jnp.sum(jnp.where(mine, marks[b], 0.0), axis=1, keepdims=True)
            mbuf[b, i * slots : (i + 1) * slots, :] = jnp.broadcast_to(mark, (slots, BLOCK))
            chosen.append(jnp.where(mine, 1.0, 0.0))
        select = jnp.concatenate(chosen, axis=0).astype(BF16)
        pbuf[i] = select
        picked = jnp.dot(
            select, qbuf[2 * i * rows : 2 * (i + 1) * rows, :], preferred_element_type=F32
        ).astype(BF16)
        for b in range(blocks):
            gbuf[b, i * slots : (i + 1) * slots, :] = picked[b * slots : (b + 1) * slots, :]

    def one_block(b):
        rows_in = gbuf[b]
        here = pl.multiple_of(b * BLOCK, BLOCK)
        weights = w_ref[pl.ds(here, BLOCK), :]
        logits = lax.dot_general(
            rows_in, weights, (((1,), (1,)), ((), ())), preferred_element_type=F32
        )
        mark = mbuf[b]
        offsets = lax.broadcasted_iota(jnp.int32, mark.shape, 1).astype(F32) + 1.0
        target = (offsets == mark).astype(F32)
        slopes = jnp.where(mark > 0.0, jax.nn.sigmoid(logits) - target, 0.0).astype(BF16)
        wg[pl.ds(here, BLOCK), :] = lax.dot_general(
            slopes, rows_in, (((0,), (0,)), ((), ())), preferred_element_type=F32
        )
        qslot[b] = jnp.dot(slopes, weights, preferred_element_type=F32)

    part_copies = {}

    def row_parts(i):
        slot_grad = jnp.concatenate(
            [qslot[b, i * slots : (i + 1) * slots, :] for b in range(blocks)], axis=0
        )
        high = slot_grad.astype(BF16)
        low = (slot_grad - high.astype(F32)).astype(BF16)
        dims = (((0,), (0,)), ((), ()))
        part = lax.dot_general(pbuf[i], high, dims, preferred_element_type=F32)
        part = part + lax.dot_general(pbuf[i], low, dims, preferred_element_type=F32)
        own_part[i] = part[0:rows]
        pair_out[i] = part[rows : 2 * rows]
        part_copies[i] = remote(pair_out.at[i], pair_in.at[i], part_send, part_recv, i, twin)

    def pick_turn(turn):
        for way in (0, 1):
            for part in halves(way, turn):
                if (way, turn, part) in twins:
                    for copy in twins[way, turn, part]:
                        copy.wait_recv()
        pick(pair_of(0, turn))
        if 0 < turn < turns:
            pick(pair_of(1, turn))

    for part in (0, 1):
        send_on(0, 1, part)
        send_on(1, 1, part)
    for part in (0, 1):
        send_twin(0, 0, part)
    below = lax.broadcasted_iota(jnp.int32, (2 * rows, 2 * rows), 0)
    right = lax.broadcasted_iota(jnp.int32, (2 * rows, 2 * rows), 1)
    one_shard = lax.div(below, rows) == lax.div(right, rows)
    earlier[...] = jnp.where((below < right) & one_shard, 1.0, 0.0).astype(BF16)
    for turn in range(1, turns + 1):
        for part in (0, 1):
            for way in (0, 1):
                if (way, turn, part) not in gathers:
                    continue
                for copy in gathers[way, turn, part]:
                    copy.wait_recv()
                if turn < turns and part in halves(way, turn + 1):
                    send_on(way, turn + 1, part)
                send_twin(way, turn, part)
        pick_turn(turn - 1)
    pick_turn(turns)

    wg_copies = {}

    def wg_send_on(peer, y):
        low = y * piece
        start = pl.multiple_of(lax.rem(rep + 1 + peer, reps) * shard + low, piece)
        wg_out[peer, low : low + piece, :] = wg[pl.ds(start, piece), :].astype(BF16)
        wg_copies[peer, y] = remote(
            wg_out.at[peer, pl.ds(low, piece)], wg_in.at[peer, pl.ds(low, piece)],
            wg_send, wg_recv, peer * pieces + y, partners[peer],
        )

    if shard >= BLOCK:
        per_shard = shard // BLOCK
        for j in range(blocks):
            peer = j // per_shard
            one_block(lax.rem(rep + 1 + peer, reps) * per_shard + j % per_shard)
            if peer < reps - 1:
                wg_send_on(peer, j % per_shard)
    else:
        for b in range(blocks):
            one_block(b)
        for peer in range(reps - 1):
            wg_send_on(peer, 0)
    for turn in range(turns, -1, -1):
        for way in ((0,) if turn in (0, turns) else (0, 1)):
            row_parts(pair_of(way, turn))
    load_first.wait()
    load_second.wait()

    ring_copies = {}

    def ring_step(s):
        for way in (0, 1):
            i = pair_of(1 - way, turns - s)
            if s > 0 or way == 0:
                part_copies[i].wait_recv()
            k = way * turns + s
            device = ahead if way == 0 else behind
            if s == 0:
                low = half * way
                value = own_part[i, low : low + half, :] + pair_in[i, low : low + half, :]
                ring_out[k, 0:half, :] = value.astype(BF16)
                ring_copies[way, s] = remote(
                    ring_out.at[k, pl.ds(0, half)], ring_in.at[k, pl.ds(0, half)],
                    ring_send, ring_recv, k, device,
                )
                continue
            ring_copies[way, s - 1].wait_recv()
            value = own_part[i] + pair_in[i]
            if s == 1:
                low = half * way
                mixed = [value[0:half], value[half:rows]]
                mixed[way] = mixed[way] + ring_in[k - 1, 0:half, :].astype(F32)
                value = jnp.concatenate(mixed, axis=0)
            else:
                value = value + ring_in[k - 1].astype(F32)
            if s == turns - 1:
                last_out[way] = value
                ring_copies[way, s] = remote(
                    last_out.at[way], last_in.at[way], ring_send, ring_recv, k, device
                )
            else:
                ring_out[k] = value.astype(BF16)
                ring_copies[way, s] = remote(
                    ring_out.at[k], ring_in.at[k], ring_send, ring_recv, k, device
                )

    def ring_end():
        part_copies[0].wait_recv()
        value = own_part[0] + pair_in[0]
        for way in (0, 1):
            ring_copies[way, turns - 1].wait_recv()
            value = value + last_in[way]
        grad_ref[...] = value

    step_copies = []

    def adam(y):
        low = y * piece
        here = pl.multiple_of(rep * shard + low, piece)
        total = wg[pl.ds(here, piece), :]
        for peer in range(reps - 1):
            wg_copies[peer, y].wait_recv()
            total = total + wg_in[peer, low : low + piece, :].astype(F32)
        sum_ref[low : low + piece, :] = total
        new_first = beta_first * first[low : low + piece, :] + (1.0 - beta_first) * total
        new_second = beta_second * second[low : low + piece, :] + (1.0 - beta_second) * total * total
        first_hat = new_first * (1.0 / (1.0 - beta_first**step_count))
        second_hat = new_second * (1.0 / (1.0 - beta_second**step_count))
        step_ref[pl.ds(here, piece), :] = (
            first_hat / (jnp.sqrt(second_hat) + adam_epsilon)
        ).astype(BF16)
        for peer in range(reps - 1):
            step_copies.append(
                remote(
                    step_ref.at[pl.ds(here, piece)], step_ref.at[pl.ds(here, piece)],
                    step_send, step_recv, peer * pieces + y, partners[peer],
                )
            )

    ring_step(0)
    ring_step(1)
    for k in range(max(pieces, turns - 1)):
        if k < pieces:
            adam(k)
        if k + 2 < turns:
            ring_step(k + 2)
        if k + 2 == turns:
            ring_end()

    for copies in (gathers, twins):
        for group in copies.values():
            for copy in group:
                copy.wait_send()
    for copies in (part_copies, ring_copies, wg_copies):
        for copy in copies.values():
            copy.wait_send()
    for copy in step_copies:
        copy.wait_send()
        copy.wait_recv()


def body(reps, labs, queries, shortlist, positive, label_weight, first_moment, second_moment):
    rows, depth = queries.shape
    names = shortlist.shape[1]
    local = label_weight.shape[0]
    shard = first_moment.shape[1]
    chips = labs // 2
    turns = chips // 2
    blocks = local // BLOCK
    piece = min(shard, BLOCK)
    pieces = shard // piece
    info = jnp.concatenate([shortlist.T, positive.T], axis=0).astype(BF16)
    vmem = pl.BlockSpec(memory_space=pltpu.VMEM)
    anywhere = pl.BlockSpec(memory_space=pl.ANY)
    dma = pltpu.SemaphoreType.DMA
    scratch = [
        pltpu.VMEM((labs * rows, depth), BF16),
        pltpu.VMEM((labs, 2 * names, rows), BF16),
        pltpu.VMEM((local, depth), F32),
        pltpu.VMEM((blocks, labs * CAP, depth), BF16),
        pltpu.VMEM((blocks, labs * CAP, BLOCK), F32),
        pltpu.VMEM((chips, blocks * 2 * CAP, 2 * rows), BF16),
        pltpu.VMEM((blocks, labs * CAP, depth), F32),
        pltpu.VMEM((2 * rows, 2 * rows), BF16),
        pltpu.VMEM((chips, rows, depth), F32),
        pltpu.VMEM((chips, rows, depth), F32),
        pltpu.VMEM((chips, rows, depth), F32),
        pltpu.VMEM((2 * turns, rows, depth), BF16),
        pltpu.VMEM((2 * turns, rows, depth), BF16),
        pltpu.VMEM((2, rows, depth), F32),
        pltpu.VMEM((2, rows, depth), F32),
        pltpu.VMEM((reps - 1, shard, depth), BF16),
        pltpu.VMEM((reps - 1, shard, depth), BF16),
        pltpu.VMEM((shard, depth), F32),
        pltpu.VMEM((shard, depth), F32),
    ]
    scratch += [dma((4 * turns + 2,))] * 8
    scratch += [dma((chips,))] * 2 + [dma((2 * turns,))] * 2
    scratch += [dma(((reps - 1) * pieces,))] * 4 + [dma((2,))]
    grad, step, total = pl.pallas_call(
        functools.partial(kernel, reps, labs, rows, depth, names, local, shard),
        out_shape=(
            jax.ShapeDtypeStruct((rows, depth), F32),
            jax.ShapeDtypeStruct((local, depth), BF16),
            jax.ShapeDtypeStruct((shard, depth), F32),
        ),
        in_specs=[vmem, vmem, vmem, anywhere, anywhere],
        out_specs=(vmem, vmem, vmem),
        scratch_shapes=scratch,
        compiler_params=pltpu.CompilerParams(
            collective_id=0, has_side_effects=True, vmem_limit_bytes=56 * 1024 * 1024
        ),
    )(queries, info, label_weight, first_moment[0], second_moment[0])
    total = total[None]
    new_first = beta_first * first_moment + (1.0 - beta_first) * total
    new_second = beta_second * second_moment + (1.0 - beta_second) * total * total
    new_weight = label_weight.astype(F32) - learn_rate * step.astype(F32)
    return (grad, new_weight, new_first, new_second)


def solution(mesh):
    in_specs = (
        P(("rep", "lab"), None),
        P(("rep", "lab"), None),
        P(("rep", "lab"), None),
        P("lab", None),
        P("rep", "lab", None),
        P("rep", "lab", None),
    )
    out_specs = (
        P(("rep", "lab"), None),
        P("lab", None),
        P("rep", "lab", None),
        P("rep", "lab", None),
    )
    run = functools.partial(body, mesh.shape["rep"], mesh.shape["lab"])
    return jax.shard_map(run, mesh=mesh, in_specs=in_specs, out_specs=out_specs, check_vma=False)
```

time: 76.6 us -> 77.3 us (level)
  no operation moved by 1% of the time
where the time goes in v2:
time: 77.3 us; the launch traced here: 77.1 us
  Pallas kernels  68.6 us (89%)
  other arithmetic  7.05 us (9%)
    pallas_call x1, Pallas kernels, body(): pl.pallas_call(functools.partial(kernel, reps, labs, rows, depth, names,...  68.6 us
    sub x1, other arithmetic, body(): new_weight = label_weight.astype(F32) - learn_rate * step.astype(F32)  3.63 us
    add x1, other arithmetic, body(): beta_second * second_moment + (1.0 - beta_second) * total * total  2.12 us

profile of v2, /device:TPU:0, one launch (start us, length us, event | category | flops | bytes accessed | tf_op | source)
XLA Modules:
  0.0 77.1 jit_solution(13337724793437610608)
XLA Ops:
  0.6 0.7 convert_bitcast_fusion
  1.3 0.6 pad_maximum_fusion.info_ref
  1.9 0.0 copy-start
  1.9 68.6 %shard_map.93 = (f32[128,768]{1,0:T(8,128)}, bf16[1024,768]{1,0:T(8,128)(2,1)}, f32[512,768]{1,0:T(8,128)}) custom-call(bf16[128,768]{1,0:T(8,128)(2,1)} %q_ref.1, bf16[16,128]{1,0:T(8,128)(2,1)} %pad_maximum_fusion.info_ref, bf16[1024,768]{1,0:T(8,128)(2,1)} %w_ref.1, f32[512,768]{1,0:T(8,128)} %bitcast.12, f32[512,768]{1,0:T(8,128)} %bitcast.13), custom_call_target="tpu_custom_call" | custom-call | tf_op jit(solution)/shard_map/pallas_call | solution.py:380
  70.5 0.0 copy-done
  70.5 0.0 copy-start.1
  70.5 0.0 copy-start.2
  70.5 0.0 copy-start.3
  70.6 3.6 %multiply_subtract_fusion = f32[1024,768]{1,0:T(8,128)} fusion(bf16[1024,768]{1,0:T(8,128)(2,1)} %get-tuple-element.8, bf16[1024,768]{1,0:T(8,128)(2,1)S(1)} %copy-done), kind=kLoop, calls=%fused_computation | loop fusion | flops 3145728 | bytes 6291456 | tf_op jit(solution)/shard_map/sub | solution.py:397
  74.2 0.0 copy-done.1
  74.2 0.0 copy-done.2
  74.2 0.0 copy-done.3
  74.2 0.0 copy-start.4
  74.2 2.1 %fusion.1 = (f32[1,512,768]{2,1,0:T(8,128)}, f32[1,512,768]{2,1,0:T(8,128)}) fusion(f32[512,768]{1,0:T(8,128)S(1)} %copy-done.3, f32[1,512,768]{2,1,0:T(8,128)S(1)} %copy-done.2, f32[1,512,768]{2,1,0:T(8,128)S(1)} %copy-done.1), kind=kLoop, calls=%fused_computation.3 | loop fusion | flops 2752512 | bytes 7864320 | tf_op jit(solution)/shard_map/add | solution.py:396
  76.3 0.0 copy-done.4
  76.3 0.7 copy.11
Async XLA Ops:
  1.9 68.6 %copy-start = (bf16[1024,768]{1,0:T(8,128)(2,1)S(1)}, bf16[1024,768]{1,0:T(8,128)(2,1)}, u32[]{:S(2)}) copy-start(bf16[1024,768]{1,0:T(8,128)(2,1)} %w_ref.1) | copy-start | bytes 4718596
  70.5 3.7 %copy-start.1 = (f32[1,512,768]{2,1,0:T(8,128)S(1)}, f32[1,512,768]{2,1,0:T(8,128)}, u32[]{:S(2)}) copy-start(f32[1,512,768]{2,1,0:T(8,128)} %param.10) | copy-start | bytes 4718596
  70.5 3.7 %copy-start.2 = (f32[1,512,768]{2,1,0:T(8,128)S(1)}, f32[1,512,768]{2,1,0:T(8,128)}, u32[]{:S(2)}) copy-start(f32[1,512,768]{2,1,0:T(8,128)} %param.11) | copy-start | bytes 4718596
  70.5 3.6 %copy-start.3 = (f32[512,768]{1,0:T(8,128)S(1)}, f32[512,768]{1,0:T(8,128)}, u32[]{:S(2)}) copy-start(f32[512,768]{1,0:T(8,128)} %get-tuple-element.9) | copy-start | bytes 4718596
  74.2 2.1 %copy-start.4 = (f32[128,768]{1,0:T(8,128)S(1)}, f32[128,768]{1,0:T(8,128)}, u32[]{:S(2)}) copy-start(f32[128,768]{1,0:T(8,128)} %get-tuple-element.18) | copy-start | bytes 1179652

commit v3 on v2

--- a/solution.py
+++ b/solution.py
@@ -26,16 +26,22 @@
     return 2 * place + back * (2 * (chips - 1 - place) + 1 - 2 * place)
 
 
+def mirrored(reps, shard):
+    return reps == 2 and shard % BLOCK == 0
+
+
 def kernel(
     reps, labs, rows, depth, names, local, shard,
     q_ref, info_ref, w_ref, first_ref, second_ref,
     grad_ref, step_ref, sum_ref,
     qbuf, ibuf, wg, gbuf, mbuf, pbuf, qslot, earlier, own_part, pair_out, pair_in,
     ring_out, ring_in, last_out, last_in, wg_out, wg_in, first, second,
+    far_q, far_i, far_g, far_m,
     gather_send, gather_recv, note_send, note_recv,
     twin_send, twin_recv, twin_note_send, twin_note_recv,
     part_send, part_recv, ring_send, ring_recv,
     wg_send, wg_recv, step_send, step_recv, load_sem,
+    cross_send, cross_recv, cross_note_send, cross_note_recv,
 ):
     chips = labs // 2
     turns = chips // 2
@@ -86,89 +92,123 @@
     def sem(way, turn):
         return 2 * turn - 1 + way if turn else 0
 
+    mirror = mirrored(reps, shard)
+    own_first = rep * (shard // BLOCK)
+    crossing = (0, 1, turns - 1)
+    both = ((qbuf, ibuf, 0), (far_q, far_i, 4 * turns + 2))
     gathers, twins = {}, {}
     slots = 2 * CAP
 
     def halves(way, turn):
         return (way,) if turn == turns else (0, 1)
 
-    def send_on(way, turn, part):
+    def send_on(way, turn, part, far=0):
+        qb, ib, base = both[far]
         src, dst = chunk(way, turn - 1), chunk(way, turn)
-        k = 2 * sem(way, turn) + part
+        k = base + 2 * sem(way, turn) + part
         device = ahead if way == 0 else behind
         low = part * half
         got = [
             remote(
-                qbuf.at[pl.ds(src * rows + low, half)], qbuf.at[pl.ds(dst * rows + low, half)],
+                qb.at[pl.ds(src * rows + low, half)], qb.at[pl.ds(dst * rows + low, half)],
                 gather_send, gather_recv, k, device,
             )
         ]
         if part == 0:
-            got.append(remote(ibuf.at[src], ibuf.at[dst], note_send, note_recv, k, device))
-        gathers[way, turn, part] = got
-
-    def send_twin(way, turn, part):
+            got.append(remote(ib.at[src], ib.at[dst], note_send, note_recv, k, device))
+        gathers[way, turn, part, far] = got
+
+    def send_across(way, turn, part):
         c = chunk(way, turn)
         k = 2 * sem(way, turn) + part
+        here = pl.ds(c * rows + part * half, half)
+        got = [remote(qbuf.at[here], far_q.at[here], cross_send, cross_recv, k, partners[0])]
+        if part == 0:
+            got.append(
+                remote(ibuf.at[c], far_i.at[c], cross_note_send, cross_note_recv, k, partners[0])
+            )
+        gathers[way, turn, part, 1] = got
+
+    def send_twin(way, turn, part, far=0):
+        qb, ib, base = both[far]
+        c = chunk(way, turn)
+        k = base + 2 * sem(way, turn) + part
         low = part * half
         got = [
             remote(
-                qbuf.at[pl.ds(c * rows + low, half)], qbuf.at[pl.ds((c + 1) * rows + low, half)],
+                qb.at[pl.ds(c * rows + low, half)], qb.at[pl.ds((c + 1) * rows + low, half)],
                 twin_send, twin_recv, k, twin,
             )
         ]
         if part == 0:
-            got.append(remote(ibuf.at[c], ibuf.at[c + 1], twin_note_send, twin_note_recv, k, twin))
-        twins[way, turn, part] = got
+            got.append(remote(ib.at[c], ib.at[c + 1], twin_note_send, twin_note_recv, k, twin))
+        twins[way, turn, part, far] = got
 
     def pair_of(way, turn):
         return chunk(way, turn) // 2
 
-    def pick(i):
+    def pick(i, far=0):
+        qb, ib, _ = both[far]
+        count = shard // BLOCK if far else blocks
+        block0 = lab * blocks + (own_first if far else 0)
+        gb, mb = (far_g, far_m) if far else (gbuf, mbuf)
         width = 2 * rows
         pair = (2 * i, 2 * i + 1)
-        listed = jnp.concatenate([ibuf[c, 0:names, :] for c in pair], axis=1).astype(F32)
-        wanted = jnp.concatenate([ibuf[c, names : 2 * names, :] for c in pair], axis=1).astype(F32)
+        listed = jnp.concatenate([ib[c, 0:names, :] for c in pair], axis=1).astype(F32)
+        wanted = jnp.concatenate([ib[c, names : 2 * names, :] for c in pair], axis=1).astype(F32)
         hits, marks = [], []
-        for b in range(blocks):
-            same = listed == (lab * blocks + b).astype(F32)
+        for b in range(count):
+            same = listed == (block0 + b).astype(F32)
             hits.append(jnp.sum(jnp.where(same, 1.0, 0.0), axis=0, keepdims=True))
             marks.append(jnp.sum(jnp.where(same, wanted + 1.0, 0.0), axis=0, keepdims=True))
         hit = jnp.concatenate(hits, axis=0)
-        later = lax.broadcasted_iota(jnp.int32, (blocks, width), 1) >= rows
+        later = lax.broadcasted_iota(jnp.int32, (count, width), 1) >= rows
         order = jnp.dot(hit.astype(BF16), earlier[...], preferred_element_type=F32)
         order = order + jnp.where(later, float(CAP), 0.0)
         order = jnp.where(hit > 0.0, order, -1.0)
         number = lax.broadcasted_iota(jnp.int32, (slots, width), 0).astype(F32)
         chosen = []
-        for b in range(blocks):
+        for b in range(count):
             mine = number == order[b : b + 1, :]
             mark = jnp.sum(jnp.where(mine, marks[b], 0.0), axis=1, keepdims=True)
-            mbuf[b, i * slots : (i + 1) * slots, :] = jnp.broadcast_to(mark, (slots, BLOCK))
+            mb[b, i * slots : (i + 1) * slots, :] = jnp.broadcast_to(mark, (slots, BLOCK))
             chosen.append(jnp.where(mine, 1.0, 0.0))
         select = jnp.concatenate(chosen, axis=0).astype(BF16)
-        pbuf[i] = select
+        if not far:
+            pbuf[i] = select
         picked = jnp.dot(
-            select, qbuf[2 * i * rows : 2 * (i + 1) * rows, :], preferred_element_type=F32
+            select, qb[2 * i * rows : 2 * (i + 1) * rows, :], preferred_element_type=F32
         ).astype(BF16)
-        for b in range(blocks):
-            gbuf[b, i * slots : (i + 1) * slots, :] = picked[b * slots : (b + 1) * slots, :]
-
-    def one_block(b):
+        for b in range(count):
+            gb[b, i * slots : (i + 1) * slots, :] = picked[b * slots : (b + 1) * slots, :]
+
+    def slopes_of(rows_in, weights, mark):
+        logits = lax.dot_general(
+            rows_in, weights, (((1,), (1,)), ((), ())), preferred_element_type=F32
+        )
+        offsets = lax.broadcasted_iota(jnp.int32, mark.shape, 1).astype(F32) + 1.0
+        target = (offsets == mark).astype(F32)
+        return jnp.where(mark > 0.0, jax.nn.sigmoid(logits) - target, 0.0).astype(BF16)
+
+    def weight_part(slopes, rows_in):
+        return lax.dot_general(
+            slopes, rows_in, (((0,), (0,)), ((), ())), preferred_element_type=F32
+        )
+
+    def one_block(b, with_weights=True):
         rows_in = gbuf[b]
         here = pl.multiple_of(b * BLOCK, BLOCK)
         weights = w_ref[pl.ds(here, BLOCK), :]
-        logits = lax.dot_general(
-            rows_in, weights, (((1,), (1,)), ((), ())), preferred_element_type=F32
-        )
-        mark = mbuf[b]
-        offsets = lax.broadcasted_iota(jnp.int32, mark.shape, 1).astype(F32) + 1.0
-        target = (offsets == mark).astype(F32)
-        slopes = jnp.where(mark > 0.0, jax.nn.sigmoid(logits) - target, 0.0).astype(BF16)
-        wg[pl.ds(here, BLOCK), :] = lax.dot_general(
-            slopes, rows_in, (((0,), (0,)), ((), ())), preferred_element_type=F32
-        )
+        slopes = slopes_of(rows_in, weights, mbuf[b])
+        if with_weights:
+            wg[pl.ds(here, BLOCK), :] = weight_part(slopes, rows_in)
         qslot[b] = jnp.dot(slopes, weights, preferred_element_type=F32)
+
+    def far_block(j):
+        rows_in = far_g[j]
+        here = pl.multiple_of((own_first + j) * BLOCK, BLOCK)
+        slopes = slopes_of(rows_in, w_ref[pl.ds(here, BLOCK), :], far_m[j])
+        wg[pl.ds(here, BLOCK), :] = wg[pl.ds(here, BLOCK), :] + weight_part(slopes, rows_in)
 
     part_copies = {}
 
@@ -185,19 +225,41 @@
         pair_out[i] = part[rows : 2 * rows]
         part_copies[i] = remote(pair_out.at[i], pair_in.at[i], part_send, part_recv, i, twin)
 
-    def pick_turn(turn):
+    def pick_turn(turn, far=0):
         for way in (0, 1):
             for part in halves(way, turn):
-                if (way, turn, part) in twins:
-                    for copy in twins[way, turn, part]:
+                if (way, turn, part, far) in twins:
+                    for copy in twins[way, turn, part, far]:
                         copy.wait_recv()
-        pick(pair_of(0, turn))
+        pick(pair_of(0, turn), far)
         if 0 < turn < turns:
-            pick(pair_of(1, turn))
+            pick(pair_of(1, turn), far)
+
+    in_order = ((0, 0), (1, 1), (0, 1), (1, 0))
+
+    def cross_turn(turn):
+        for way, part in in_order:
+            if turn or not way:
+                send_across(way, turn, part)
+
+    def far_arrived(turn, cases=in_order):
+        for way, part in cases:
+            if (way, turn, part, 1) not in gathers:
+                continue
+            for copy in gathers[way, turn, part, 1]:
+                copy.wait_recv()
+            following = turn + 1
+            if following <= turns and following not in crossing:
+                for on in (0, 1) if turn == 0 else (way,):
+                    if part in halves(on, following):
+                        send_on(on, following, part, 1)
+            send_twin(way, turn, part, 1)
 
     for part in (0, 1):
         send_on(0, 1, part)
         send_on(1, 1, part)
+    if mirror:
+        cross_turn(0)
     for part in (0, 1):
         send_twin(0, 0, part)
     below = lax.broadcasted_iota(jnp.int32, (2 * rows, 2 * rows), 0)
@@ -207,14 +269,21 @@
     for turn in range(1, turns + 1):
         for part in (0, 1):
             for way in (0, 1):
-                if (way, turn, part) not in gathers:
+                if (way, turn, part, 0) not in gathers:
                     continue
-                for copy in gathers[way, turn, part]:
+                for copy in gathers[way, turn, part, 0]:
                     copy.wait_recv()
                 if turn < turns and part in halves(way, turn + 1):
                     send_on(way, turn + 1, part)
                 send_twin(way, turn, part)
+        if mirror and turn in crossing:
+            cross_turn(turn)
         pick_turn(turn - 1)
+        if mirror and turn == turns - 1:
+            for far_turn in (0, 1):
+                far_arrived(far_turn)
+    if mirror:
+        far_arrived(turns - 1, in_order[0:2])
     pick_turn(turns)
 
     wg_copies = {}
@@ -228,7 +297,12 @@
             wg_send, wg_recv, peer * pieces + y, partners[peer],
         )
 
-    if shard >= BLOCK:
+    if mirror:
+        per_shard = shard // BLOCK
+        for j in range(blocks):
+            peer = j // per_shard
+            one_block(lax.rem(rep + 1 + peer, reps) * per_shard + j % per_shard, peer > 0)
+    elif shard >= BLOCK:
         per_shard = shard // BLOCK
         for j in range(blocks):
             peer = j // per_shard
@@ -298,7 +372,7 @@
         low = y * piece
         here = pl.multiple_of(rep * shard + low, piece)
         total = wg[pl.ds(here, piece), :]
-        for peer in range(reps - 1):
+        for peer in range(0 if mirror else reps - 1):
             wg_copies[peer, y].wait_recv()
             total = total + wg_in[peer, low : low + piece, :].astype(F32)
         sum_ref[low : low + piece, :] = total
@@ -318,9 +392,23 @@
             )
 
     ring_step(0)
+    if mirror:
+        pick_turn(0, 1)
+        pick_turn(1, 1)
+        far_arrived(turns - 1, in_order[2:4])
+        for turn in range(2, turns - 1):
+            far_arrived(turn)
+        far_arrived(turns)
+        for turn in range(2, turns + 1):
+            pick_turn(turn, 1)
+        far_block(0)
+        adam(0)
     ring_step(1)
     for k in range(max(pieces, turns - 1)):
-        if k < pieces:
+        if mirror and k + 1 < pieces:
+            far_block(k + 1)
+            adam(k + 1)
+        if not mirror and k < pieces:
             adam(k)
         if k + 2 < turns:
             ring_step(k + 2)
@@ -374,9 +462,17 @@
         pltpu.VMEM((shard, depth), F32),
         pltpu.VMEM((shard, depth), F32),
     ]
-    scratch += [dma((4 * turns + 2,))] * 8
+    far_labs, far_blocks = (labs, shard // BLOCK) if mirrored(reps, shard) else (1, 1)
+    scratch += [
+        pltpu.VMEM((far_labs * rows, depth), BF16),
+        pltpu.VMEM((far_labs, 2 * names, rows), BF16),
+        pltpu.VMEM((far_blocks, far_labs * CAP, depth), BF16),
+        pltpu.VMEM((far_blocks, far_labs * CAP, BLOCK), F32),
+    ]
+    scratch += [dma((8 * turns + 4,))] * 8
     scratch += [dma((chips,))] * 2 + [dma((2 * turns,))] * 2
     scratch += [dma(((reps - 1) * pieces,))] * 4 + [dma((2,))]
+    scratch += [dma((4 * turns + 2,))] * 4
     grad, step, total = pl.pallas_call(
         functools.partial(kernel, reps, labs, rows, depth, names, local, shard),
         out_shape=(

time: 77.3 us -> 75.7 us (0.979)
  Pallas kernels: 68.6 us -> 66.9 us
    pallas_call x1, Pallas kernels: 68.6 us -> 66.9 us  [body(): pl.pallas_call(functools.partial(kernel, reps, labs, rows, depth, names,...]
where the time goes in v3:
time: 75.7 us; the launch traced here: 75.5 us
  Pallas kernels  66.9 us (88%)
  other arithmetic  7.05 us (9%)
  local copies, waits for them, and re-layouts  0.77 us (1%)
    pallas_call x1, Pallas kernels, body(): pl.pallas_call(functools.partial(kernel, reps, labs, rows, depth, names,...  66.9 us
    sub x1, other arithmetic, body(): new_weight = label_weight.astype(F32) - learn_rate * step.astype(F32)  3.63 us
    add x1, other arithmetic, body(): beta_second * second_moment + (1.0 - beta_second) * total * total  2.12 us

profile of v3, /device:TPU:0, one launch (start us, length us, event | category | flops | bytes accessed | tf_op | source)
XLA Modules:
  0.0 75.5 jit_solution(11105372024987800330)
XLA Ops:
  0.6 0.7 convert_bitcast_fusion
  1.3 0.6 pad_maximum_fusion.info_ref
  1.9 0.0 copy-start
  1.9 66.9 %shard_map.93 = (f32[128,768]{1,0:T(8,128)}, bf16[1024,768]{1,0:T(8,128)(2,1)}, f32[512,768]{1,0:T(8,128)}) custom-call(bf16[128,768]{1,0:T(8,128)(2,1)} %q_ref.1, bf16[16,128]{1,0:T(8,128)(2,1)} %pad_maximum_fusion.info_ref, bf16[1024,768]{1,0:T(8,128)(2,1)} %w_ref.1, f32[512,768]{1,0:T(8,128)} %bitcast.12, f32[512,768]{1,0:T(8,128)} %bitcast.13), custom_call_target="tpu_custom_call" | custom-call | tf_op jit(solution)/shard_map/pallas_call | solution.py:476
  68.9 0.0 copy-done
  68.9 0.0 copy-start.1
  68.9 0.0 copy-start.2
  68.9 0.0 copy-start.3
  68.9 3.6 %multiply_subtract_fusion = f32[1024,768]{1,0:T(8,128)} fusion(bf16[1024,768]{1,0:T(8,128)(2,1)} %get-tuple-element.8, bf16[1024,768]{1,0:T(8,128)(2,1)S(1)} %copy-done), kind=kLoop, calls=%fused_computation | loop fusion | flops 3145728 | bytes 6291456 | tf_op jit(solution)/shard_map/sub | solution.py:493
  72.6 0.0 copy-done.1
  72.6 0.0 copy-done.2
  72.6 0.0 copy-done.3
  72.6 0.0 copy-start.4
  72.6 2.1 %fusion.1 = (f32[1,512,768]{2,1,0:T(8,128)}, f32[1,512,768]{2,1,0:T(8,128)}) fusion(f32[512,768]{1,0:T(8,128)S(1)} %copy-done.3, f32[1,512,768]{2,1,0:T(8,128)S(1)} %copy-done.2, f32[1,512,768]{2,1,0:T(8,128)S(1)} %copy-done.1), kind=kLoop, calls=%fused_computation.3 | loop fusion | flops 2752512 | bytes 7864320 | tf_op jit(solution)/shard_map/add | solution.py:492
  74.7 0.0 copy-done.4
  74.7 0.7 copy.11
Async XLA Ops:
  1.9 67.0 %copy-start = (bf16[1024,768]{1,0:T(8,128)(2,1)S(1)}, bf16[1024,768]{1,0:T(8,128)(2,1)}, u32[]{:S(2)}) copy-start(bf16[1024,768]{1,0:T(8,128)(2,1)} %w_ref.1) | copy-start | bytes 4718596
  68.9 3.7 %copy-start.1 = (f32[1,512,768]{2,1,0:T(8,128)S(1)}, f32[1,512,768]{2,1,0:T(8,128)}, u32[]{:S(2)}) copy-start(f32[1,512,768]{2,1,0:T(8,128)} %param.10) | copy-start | bytes 4718596
  68.9 3.7 %copy-start.2 = (f32[1,512,768]{2,1,0:T(8,128)S(1)}, f32[1,512,768]{2,1,0:T(8,128)}, u32[]{:S(2)}) copy-start(f32[1,512,768]{2,1,0:T(8,128)} %param.11) | copy-start | bytes 4718596
  68.9 3.6 %copy-start.3 = (f32[512,768]{1,0:T(8,128)S(1)}, f32[512,768]{1,0:T(8,128)}, u32[]{:S(2)}) copy-start(f32[512,768]{1,0:T(8,128)} %get-tuple-element.9) | copy-start | bytes 4718596
  72.6 2.1 %copy-start.4 = (f32[128,768]{1,0:T(8,128)S(1)}, f32[128,768]{1,0:T(8,128)}, u32[]{:S(2)}) copy-start(f32[128,768]{1,0:T(8,128)} %get-tuple-element.18) | copy-start | bytes 1179652

commit v4 on v3

--- a/solution.py
+++ b/solution.py
@@ -94,7 +94,6 @@
 
     mirror = mirrored(reps, shard)
     own_first = rep * (shard // BLOCK)
-    crossing = (0, 1, turns - 1)
     both = ((qbuf, ibuf, 0), (far_q, far_i, 4 * turns + 2))
     gathers, twins = {}, {}
     slots = 2 * CAP
@@ -195,14 +194,20 @@
             slopes, rows_in, (((0,), (0,)), ((), ())), preferred_element_type=F32
         )
 
-    def one_block(b, with_weights=True):
-        rows_in = gbuf[b]
+    early = (chips - 1) * slots
+
+    def one_block(b, late, with_weights=True):
+        low, high = (early, chips * slots) if late else (0, early)
+        rows_in = gbuf[b, low:high, :]
         here = pl.multiple_of(b * BLOCK, BLOCK)
         weights = w_ref[pl.ds(here, BLOCK), :]
-        slopes = slopes_of(rows_in, weights, mbuf[b])
+        slopes = slopes_of(rows_in, weights, mbuf[b, low:high, :])
         if with_weights:
-            wg[pl.ds(here, BLOCK), :] = weight_part(slopes, rows_in)
-        qslot[b] = jnp.dot(slopes, weights, preferred_element_type=F32)
+            part = weight_part(slopes, rows_in)
+            if late:
+                part = wg[pl.ds(here, BLOCK), :] + part
+            wg[pl.ds(here, BLOCK), :] = part
+        qslot[b, low:high, :] = jnp.dot(slopes, weights, preferred_element_type=F32)
 
     def far_block(j):
         rows_in = far_g[j]
@@ -237,9 +242,12 @@
 
     in_order = ((0, 0), (1, 1), (0, 1), (1, 0))
 
+    def crosses(turn, part):
+        return turn in (0, 1, turns - 1) or (turn < turns and part == 1)
+
     def cross_turn(turn):
         for way, part in in_order:
-            if turn or not way:
+            if (turn or not way) and crosses(turn, part):
                 send_across(way, turn, part)
 
     def far_arrived(turn, cases=in_order):
@@ -249,7 +257,7 @@
             for copy in gathers[way, turn, part, 1]:
                 copy.wait_recv()
             following = turn + 1
-            if following <= turns and following not in crossing:
+            if following <= turns and not crosses(following, part):
                 for on in (0, 1) if turn == 0 else (way,):
                     if part in halves(on, following):
                         send_on(on, following, part, 1)
@@ -266,6 +274,16 @@
     right = lax.broadcasted_iota(jnp.int32, (2 * rows, 2 * rows), 1)
     one_shard = lax.div(below, rows) == lax.div(right, rows)
     earlier[...] = jnp.where((below < right) & one_shard, 1.0, 0.0).astype(BF16)
+    per_shard = max(shard // BLOCK, 1)
+
+    def block_at(j):
+        if shard < BLOCK:
+            return j
+        return lax.rem(rep + 1 + j // per_shard, reps) * per_shard + j % per_shard
+
+    def needed(j):
+        return not mirror or j // per_shard > 0
+
     for turn in range(1, turns + 1):
         for part in (0, 1):
             for way in (0, 1):
@@ -276,14 +294,20 @@
                 if turn < turns and part in halves(way, turn + 1):
                     send_on(way, turn + 1, part)
                 send_twin(way, turn, part)
-        if mirror and turn in crossing:
+        if mirror and turn < turns:
             cross_turn(turn)
-        pick_turn(turn - 1)
-        if mirror and turn == turns - 1:
-            for far_turn in (0, 1):
-                far_arrived(far_turn)
-    if mirror:
-        far_arrived(turns - 1, in_order[0:2])
+        if turn < turns:
+            pick_turn(turn - 1)
+        if turn == turns - 1:
+            if mirror:
+                for far_turn in (0, 1):
+                    far_arrived(far_turn)
+            pick_turn(turn)
+            for j in range(blocks):
+                one_block(block_at(j), False, needed(j))
+            for back in range(turns - 1, -1, -1):
+                for way in (0, 1) if back else (0,):
+                    row_parts(pair_of(way, back))
     pick_turn(turns)
 
     wg_copies = {}
@@ -297,72 +321,51 @@
             wg_send, wg_recv, peer * pieces + y, partners[peer],
         )
 
-    if mirror:
-        per_shard = shard // BLOCK
-        for j in range(blocks):
-            peer = j // per_shard
-            one_block(lax.rem(rep + 1 + peer, reps) * per_shard + j % per_shard, peer > 0)
-    elif shard >= BLOCK:
-        per_shard = shard // BLOCK
-        for j in range(blocks):
-            peer = j // per_shard
-            one_block(lax.rem(rep + 1 + peer, reps) * per_shard + j % per_shard)
-            if peer < reps - 1:
-                wg_send_on(peer, j % per_shard)
-    else:
-        for b in range(blocks):
-            one_block(b)
+    for j in range(blocks):
+        one_block(block_at(j), True, needed(j))
+        if not mirror and shard >= BLOCK and j // per_shard < reps - 1:
+            wg_send_on(j // per_shard, j % per_shard)
+    if shard < BLOCK:
         for peer in range(reps - 1):
             wg_send_on(peer, 0)
-    for turn in range(turns, -1, -1):
-        for way in ((0,) if turn in (0, turns) else (0, 1)):
-            row_parts(pair_of(way, turn))
+    row_parts(pair_of(0, turns))
     load_first.wait()
     load_second.wait()
 
     ring_copies = {}
 
+    ring_order = ((0, 1), (1, 0), (0, 0), (1, 1))
+
     def ring_step(s):
         for way in (0, 1):
+            if s > 0 or way == 0:
+                part_copies[pair_of(1 - way, turns - s)].wait_recv()
+        for way, part in ring_order:
+            if s == 0 and part != way:
+                continue
             i = pair_of(1 - way, turns - s)
-            if s > 0 or way == 0:
-                part_copies[i].wait_recv()
             k = way * turns + s
-            device = ahead if way == 0 else behind
-            if s == 0:
-                low = half * way
-                value = own_part[i, low : low + half, :] + pair_in[i, low : low + half, :]
-                ring_out[k, 0:half, :] = value.astype(BF16)
-                ring_copies[way, s] = remote(
-                    ring_out.at[k, pl.ds(0, half)], ring_in.at[k, pl.ds(0, half)],
-                    ring_send, ring_recv, k, device,
-                )
-                continue
-            ring_copies[way, s - 1].wait_recv()
-            value = own_part[i] + pair_in[i]
-            if s == 1:
-                low = half * way
-                mixed = [value[0:half], value[half:rows]]
-                mixed[way] = mixed[way] + ring_in[k - 1, 0:half, :].astype(F32)
-                value = jnp.concatenate(mixed, axis=0)
+            here = pl.ds(part * half, half)
+            value = own_part[i, here, :] + pair_in[i, here, :]
+            if (way, s - 1, part) in ring_copies:
+                ring_copies[way, s - 1, part].wait_recv()
+                value = value + ring_in[k - 1, here, :].astype(F32)
+            if s == turns - 1:
+                last_out[way, here, :] = value
+                src, dst = last_out.at[way, here], last_in.at[way, here]
             else:
-                value = value + ring_in[k - 1].astype(F32)
-            if s == turns - 1:
-                last_out[way] = value
-                ring_copies[way, s] = remote(
-                    last_out.at[way], last_in.at[way], ring_send, ring_recv, k, device
-                )
-            else:
-                ring_out[k] = value.astype(BF16)
-                ring_copies[way, s] = remote(
-                    ring_out.at[k], ring_in.at[k], ring_send, ring_recv, k, device
-                )
+                ring_out[k, here, :] = value.astype(BF16)
+                src, dst = ring_out.at[k, here], ring_in.at[k, here]
+            ring_copies[way, s, part] = remote(
+                src, dst, ring_send, ring_recv, 2 * k + part, ahead if way == 0 else behind
+            )
 
     def ring_end():
         part_copies[0].wait_recv()
         value = own_part[0] + pair_in[0]
         for way in (0, 1):
-            ring_copies[way, turns - 1].wait_recv()
+            for part in (0, 1):
+                ring_copies[way, turns - 1, part].wait_recv()
             value = value + last_in[way]
         grad_ref[...] = value
 
@@ -395,25 +398,31 @@
     if mirror:
         pick_turn(0, 1)
         pick_turn(1, 1)
-        far_arrived(turns - 1, in_order[2:4])
+    ring_step(1)
+    if mirror:
+        far_arrived(turns - 1, in_order[0:2])
         for turn in range(2, turns - 1):
             far_arrived(turn)
+        far_arrived(turns - 1, in_order[2:4])
+        for turn in range(2, turns):
+            pick_turn(turn, 1)
+        ring_step(2)
         far_arrived(turns)
-        for turn in range(2, turns + 1):
-            pick_turn(turn, 1)
-        far_block(0)
-        adam(0)
-    ring_step(1)
-    for k in range(max(pieces, turns - 1)):
-        if mirror and k + 1 < pieces:
-            far_block(k + 1)
-            adam(k + 1)
-        if not mirror and k < pieces:
-            adam(k)
-        if k + 2 < turns:
-            ring_step(k + 2)
-        if k + 2 == turns:
-            ring_end()
+        pick_turn(turns, 1)
+        for y in range(pieces):
+            far_block(y)
+            adam(y)
+        for s in range(3, turns):
+            ring_step(s)
+        ring_end()
+    else:
+        for k in range(max(pieces, turns - 1)):
+            if k < pieces:
+                adam(k)
+            if k + 2 < turns:
+                ring_step(k + 2)
+            if k + 2 == turns:
+                ring_end()
 
     for copies in (gathers, twins):
         for group in copies.values():
@@ -470,7 +479,7 @@
         pltpu.VMEM((far_blocks, far_labs * CAP, BLOCK), F32),
     ]
     scratch += [dma((8 * turns + 4,))] * 8
-    scratch += [dma((chips,))] * 2 + [dma((2 * turns,))] * 2
+    scratch += [dma((chips,))] * 2 + [dma((4 * turns,))] * 2
     scratch += [dma(((reps - 1) * pieces,))] * 4 + [dma((2,))]
     scratch += [dma((4 * turns + 2,))] * 4
     grad, step, total = pl.pallas_call(

time: 75.7 us -> 81.3 us (1.074)
  Pallas kernels: 66.9 us -> 72.5 us
    pallas_call x1, Pallas kernels: 66.9 us -> 72.5 us  [body(): pl.pallas_call(functools.partial(kernel, reps, labs, rows, depth, names,...]
where the time goes in v4:
time: 81.3 us; the launch traced here: 81 us
  Pallas kernels  72.5 us (89%)
  other arithmetic  7.05 us (9%)
    pallas_call x1, Pallas kernels, body(): pl.pallas_call(functools.partial(kernel, reps, labs, rows, depth, names,...  72.5 us
    sub x1, other arithmetic, body(): new_weight = label_weight.astype(F32) - learn_rate * step.astype(F32)  3.63 us
    add x1, other arithmetic, body(): beta_second * second_moment + (1.0 - beta_second) * total * total  2.12 us

profile of v4, /device:TPU:0, one launch (start us, length us, event | category | flops | bytes accessed | tf_op | source)
XLA Modules:
  0.0 81.0 jit_solution(1132172124974498837)
XLA Ops:
  0.6 0.7 convert_bitcast_fusion
  1.3 0.6 pad_maximum_fusion.info_ref
  1.9 0.0 copy-start
  1.9 72.5 %shard_map.93 = (f32[128,768]{1,0:T(8,128)}, bf16[1024,768]{1,0:T(8,128)(2,1)}, f32[512,768]{1,0:T(8,128)}) custom-call(bf16[128,768]{1,0:T(8,128)(2,1)} %q_ref.1, bf16[16,128]{1,0:T(8,128)(2,1)} %pad_maximum_fusion.info_ref, bf16[1024,768]{1,0:T(8,128)(2,1)} %w_ref.1, f32[512,768]{1,0:T(8,128)} %bitcast.12, f32[512,768]{1,0:T(8,128)} %bitcast.13), custom_call_target="tpu_custom_call" | custom-call | tf_op jit(solution)/shard_map/pallas_call | solution.py:485
  74.4 0.0 copy-done
  74.4 0.0 copy-start.1
  74.5 0.0 copy-start.2
  74.5 0.0 copy-start.3
  74.5 3.6 %multiply_subtract_fusion = f32[1024,768]{1,0:T(8,128)} fusion(bf16[1024,768]{1,0:T(8,128)(2,1)} %get-tuple-element.8, bf16[1024,768]{1,0:T(8,128)(2,1)S(1)} %copy-done), kind=kLoop, calls=%fused_computation | loop fusion | flops 3145728 | bytes 6291456 | tf_op jit(solution)/shard_map/sub | solution.py:502
  78.1 0.0 copy-done.1
  78.1 0.0 copy-done.2
  78.1 0.0 copy-done.3
  78.1 0.0 copy-start.4
  78.1 2.1 %fusion.1 = (f32[1,512,768]{2,1,0:T(8,128)}, f32[1,512,768]{2,1,0:T(8,128)}) fusion(f32[512,768]{1,0:T(8,128)S(1)} %copy-done.3, f32[1,512,768]{2,1,0:T(8,128)S(1)} %copy-done.2, f32[1,512,768]{2,1,0:T(8,128)S(1)} %copy-done.1), kind=kLoop, calls=%fused_computation.3 | loop fusion | flops 2752512 | bytes 7864320 | tf_op jit(solution)/shard_map/add | solution.py:501
  80.3 0.0 copy-done.4
  80.3 0.7 copy.11
Async XLA Ops:
  1.9 72.5 %copy-start = (bf16[1024,768]{1,0:T(8,128)(2,1)S(1)}, bf16[1024,768]{1,0:T(8,128)(2,1)}, u32[]{:S(2)}) copy-start(bf16[1024,768]{1,0:T(8,128)(2,1)} %w_ref.1) | copy-start | bytes 4718596
  74.4 3.7 %copy-start.1 = (f32[1,512,768]{2,1,0:T(8,128)S(1)}, f32[1,512,768]{2,1,0:T(8,128)}, u32[]{:S(2)}) copy-start(f32[1,512,768]{2,1,0:T(8,128)} %param.10) | copy-start | bytes 4718596
  74.5 3.7 %copy-start.2 = (f32[1,512,768]{2,1,0:T(8,128)S(1)}, f32[1,512,768]{2,1,0:T(8,128)}, u32[]{:S(2)}) copy-start(f32[1,512,768]{2,1,0:T(8,128)} %param.11) | copy-start | bytes 4718596
  74.5 3.6 %copy-start.3 = (f32[512,768]{1,0:T(8,128)S(1)}, f32[512,768]{1,0:T(8,128)}, u32[]{:S(2)}) copy-start(f32[512,768]{1,0:T(8,128)} %get-tuple-element.9) | copy-start | bytes 4718596
  78.1 2.1 %copy-start.4 = (f32[128,768]{1,0:T(8,128)S(1)}, f32[128,768]{1,0:T(8,128)}, u32[]{:S(2)}) copy-start(f32[128,768]{1,0:T(8,128)} %get-tuple-element.18) | copy-start | bytes 1179652

commit v5 on v3

--- a/solution.py
+++ b/solution.py
@@ -314,9 +314,6 @@
             one_block(b)
         for peer in range(reps - 1):
             wg_send_on(peer, 0)
-    for turn in range(turns, -1, -1):
-        for way in ((0,) if turn in (0, turns) else (0, 1)):
-            row_parts(pair_of(way, turn))
     load_first.wait()
     load_second.wait()
 
@@ -391,29 +388,42 @@
                 )
             )
 
+    def parts_back(turn):
+        for way in (0,) if turn in (0, turns) else (0, 1):
+            row_parts(pair_of(way, turn))
+
+    parts_back(turns)
+    parts_back(turns - 1)
     ring_step(0)
+    for turn in range(turns - 2, -1, -1):
+        parts_back(turn)
     if mirror:
         pick_turn(0, 1)
         pick_turn(1, 1)
+        ring_step(1)
         far_arrived(turns - 1, in_order[2:4])
         for turn in range(2, turns - 1):
             far_arrived(turn)
+        for turn in range(2, turns):
+            pick_turn(turn, 1)
+        ring_step(2)
         far_arrived(turns)
-        for turn in range(2, turns + 1):
-            pick_turn(turn, 1)
-        far_block(0)
-        adam(0)
-    ring_step(1)
-    for k in range(max(pieces, turns - 1)):
-        if mirror and k + 1 < pieces:
-            far_block(k + 1)
-            adam(k + 1)
-        if not mirror and k < pieces:
-            adam(k)
-        if k + 2 < turns:
-            ring_step(k + 2)
-        if k + 2 == turns:
-            ring_end()
+        pick_turn(turns, 1)
+        for y in range(pieces):
+            far_block(y)
+            adam(y)
+        for s in range(3, turns):
+            ring_step(s)
+        ring_end()
+    else:
+        ring_step(1)
+        for k in range(max(pieces, turns - 1)):
+            if k < pieces:
+                adam(k)
+            if k + 2 < turns:
+                ring_step(k + 2)
+            if k + 2 == turns:
+                ring_end()
 
     for copies in (gathers, twins):
         for group in copies.values():

time: 75.7 us -> 77.2 us (1.020)
  Pallas kernels: 66.9 us -> 68.5 us
    pallas_call x1, Pallas kernels: 66.9 us -> 68.5 us  [body(): pl.pallas_call(functools.partial(kernel, reps, labs, rows, depth, names,...]
where the time goes in v5:
time: 77.2 us; the launch traced here: 77 us
  Pallas kernels  68.5 us (89%)
  other arithmetic  7.05 us (9%)
    pallas_call x1, Pallas kernels, body(): pl.pallas_call(functools.partial(kernel, reps, labs, rows, depth, names,...  68.5 us
    sub x1, other arithmetic, body(): new_weight = label_weight.astype(F32) - learn_rate * step.astype(F32)  3.63 us
    add x1, other arithmetic, body(): beta_second * second_moment + (1.0 - beta_second) * total * total  2.12 us

profile of v5, /device:TPU:0, one launch (start us, length us, event | category | flops | bytes accessed | tf_op | source)
XLA Modules:
  0.0 77.0 jit_solution(758642590487204859)
XLA Ops:
  0.6 0.7 convert_bitcast_fusion
  1.3 0.6 pad_maximum_fusion.info_ref
  1.9 0.0 copy-start
  1.9 68.5 %shard_map.93 = (f32[128,768]{1,0:T(8,128)}, bf16[1024,768]{1,0:T(8,128)(2,1)}, f32[512,768]{1,0:T(8,128)}) custom-call(bf16[128,768]{1,0:T(8,128)(2,1)} %q_ref.1, bf16[16,128]{1,0:T(8,128)(2,1)} %pad_maximum_fusion.info_ref, bf16[1024,768]{1,0:T(8,128)(2,1)} %w_ref.1, f32[512,768]{1,0:T(8,128)} %bitcast.12, f32[512,768]{1,0:T(8,128)} %bitcast.13), custom_call_target="tpu_custom_call" | custom-call | tf_op jit(solution)/shard_map/pallas_call | solution.py:486
  70.5 0.0 copy-done
  70.5 0.0 copy-start.1
  70.5 0.0 copy-start.2
  70.5 0.0 copy-start.3
  70.5 3.6 %multiply_subtract_fusion = f32[1024,768]{1,0:T(8,128)} fusion(bf16[1024,768]{1,0:T(8,128)(2,1)} %get-tuple-element.8, bf16[1024,768]{1,0:T(8,128)(2,1)S(1)} %copy-done), kind=kLoop, calls=%fused_computation | loop fusion | flops 3145728 | bytes 6291456 | tf_op jit(solution)/shard_map/sub | solution.py:503
  74.1 0.0 copy-done.1
  74.1 0.0 copy-done.2
  74.1 0.0 copy-done.3
  74.1 0.0 copy-start.4
  74.2 2.1 %fusion.1 = (f32[1,512,768]{2,1,0:T(8,128)}, f32[1,512,768]{2,1,0:T(8,128)}) fusion(f32[512,768]{1,0:T(8,128)S(1)} %copy-done.3, f32[1,512,768]{2,1,0:T(8,128)S(1)} %copy-done.2, f32[1,512,768]{2,1,0:T(8,128)S(1)} %copy-done.1), kind=kLoop, calls=%fused_computation.3 | loop fusion | flops 2752512 | bytes 7864320 | tf_op jit(solution)/shard_map/add | solution.py:502
  76.3 0.0 copy-done.4
  76.3 0.7 copy.11
Async XLA Ops:
  1.9 68.5 %copy-start = (bf16[1024,768]{1,0:T(8,128)(2,1)S(1)}, bf16[1024,768]{1,0:T(8,128)(2,1)}, u32[]{:S(2)}) copy-start(bf16[1024,768]{1,0:T(8,128)(2,1)} %w_ref.1) | copy-start | bytes 4718596
  70.5 3.7 %copy-start.1 = (f32[1,512,768]{2,1,0:T(8,128)S(1)}, f32[1,512,768]{2,1,0:T(8,128)}, u32[]{:S(2)}) copy-start(f32[1,512,768]{2,1,0:T(8,128)} %param.10) | copy-start | bytes 4718596
  70.5 3.7 %copy-start.2 = (f32[1,512,768]{2,1,0:T(8,128)S(1)}, f32[1,512,768]{2,1,0:T(8,128)}, u32[]{:S(2)}) copy-start(f32[1,512,768]{2,1,0:T(8,128)} %param.11) | copy-start | bytes 4718596
  70.5 3.6 %copy-start.3 = (f32[512,768]{1,0:T(8,128)S(1)}, f32[512,768]{1,0:T(8,128)}, u32[]{:S(2)}) copy-start(f32[512,768]{1,0:T(8,128)} %get-tuple-element.9) | copy-start | bytes 4718596
  74.1 2.1 %copy-start.4 = (f32[128,768]{1,0:T(8,128)S(1)}, f32[128,768]{1,0:T(8,128)}, u32[]{:S(2)}) copy-start(f32[128,768]{1,0:T(8,128)} %get-tuple-element.18) | copy-start | bytes 1179652
